TPU v7x, 32 devices: a whole 2x2x4 slice. The times are simulated.
32 devices in a mesh: groups: 2 (over x), slab: 16 (over z, y, core).
Axes of the slice: x: 2, y: 2, z: 4, core: 2. Of those that a mesh axis runs over, the one named last changes fastest.
Arguments:
- point_feat: bfloat16 [65536, 64], P(('groups', 'slab')), parts along dimension 0, may hold values from -6 to 6
- point_pos: float32 [3, 65536], P(None, ('groups', 'slab')), parts along dimension 1, may hold values from 0 to 128
- pair_point: int32 [32, 16, 256], P(('groups', 'slab')), parts along dimension 0, may hold values from -1 to 2044, as said below
- pair_cell: int32 [32, 16, 256], P(('groups', 'slab')), parts along dimension 0, may hold values from -1 to 131071, as said below
- lift_weight: bfloat16 [64, 64], replicated, may hold values from -0.75 to 0.75
- spectral_weight: bfloat16 [32, 32, 32, 2, 64, 64], P(None, None, 'slab'), may hold values from -28 to 28
- skip_weight: bfloat16 [64, 64], replicated, may hold values from -0.75 to 0.75
- proj_weight: bfloat16 [64, 64], replicated, may hold values from -0.75 to 0.75
Outputs:
- point_out: bfloat16 [65536, 64], P(('groups', 'slab')), parts along dimension 0
There are 2 independent parts, one for each index of `groups`. A program takes and returns all parts, laid end to end along the dimension named above; an argument that names none is the same for every part. Nothing has to cross between parts.
Inputs may be any that keep to these rules, and one draw needn't show every extreme that they name: `pair_point`: index of a point among the 2048 points of region r, or -1 in an empty slot; a slot is empty here exactly where pair_cell is -1, and the live slots of each list come first. The list of each region to its own slab is full; each region has live lists to exactly five slabs, its own among them. `pair_cell`: index (plane * 128 + y) * 128 + z of a cell within slab s, plane counted within the slab, or -1 in an empty slot.
All inputs are finite; a program needn't handle non-finite values.
Results may differ from a plain program's by a relative error of at most 0.012.
Values may be sent and summed in bfloat16 or wider, within the bound.
A program may use at most 320 MiB of HBM per device.

v0:
```python
import jax
import jax.numpy as jnp
from jax import lax
from jax.sharding import PartitionSpec as P

G = 128
C = 64
M = 32
RADIUS = 2


def mode_tables(length, modes):
    offsets = jnp.arange(modes)
    frequency = jnp.where(offsets < modes // 2, offsets, offsets - modes).astype(jnp.float32)
    places = jnp.arange(length).astype(jnp.float32)
    phase = 2.0 * jnp.pi / length * (frequency[:, None] * places[None, :])
    return (jnp.cos(phase), jnp.sin(phase))


def along(table, tensor, dimension, table_axis):
    product = jnp.tensordot(
        table, tensor, axes=((table_axis,), (dimension,)), precision=lax.Precision.HIGHEST
    )
    return jnp.moveaxis(product, 0, dimension)


def forward(real_part, imag_part, dimension, tables):
    cosine, sine = tables
    if imag_part is None:
        return (along(cosine, real_part, dimension, 1), -along(sine, real_part, dimension, 1))
    new_real = along(cosine, real_part, dimension, 1) + along(sine, imag_part, dimension, 1)
    new_imag = along(cosine, imag_part, dimension, 1) - along(sine, real_part, dimension, 1)
    return (new_real, new_imag)


def inverse(real_part, imag_part, dimension, tables, length, keep_imag):
    cosine, sine = tables
    new_real = (
        along(cosine, real_part, dimension, 0) - along(sine, imag_part, dimension, 0)
    ) / length
    if not keep_imag:
        return new_real
    new_imag = (
        along(cosine, imag_part, dimension, 0) + along(sine, real_part, dimension, 0)
    ) / length
    return (new_real, new_imag)


def mix_modes(real_part, imag_part, weights):
    real_b = real_part.astype(jnp.bfloat16)
    imag_b = imag_part.astype(jnp.bfloat16)
    first = jnp.stack([real_b, -imag_b], axis=3)
    second = jnp.stack([imag_b, real_b], axis=3)
    new_real = jnp.einsum("abcsd,abcsde->abce", first, weights, preferred_element_type=jnp.float32)
    new_imag = jnp.einsum("abcsd,abcsde->abce", second, weights, preferred_element_type=jnp.float32)
    return (new_real, new_imag)


def pair_weights(positions, cell_ids, slab_first, pair_live):
    centre_x = (cell_ids // (G * G) + slab_first).astype(jnp.float32) + 0.5
    centre_y = (cell_ids // G % G).astype(jnp.float32) + 0.5
    centre_z = (cell_ids % G).astype(jnp.float32) + 0.5
    distance = (
        (positions[0] - centre_x) ** 2
        + (positions[1] - centre_y) ** 2
        + (positions[2] - centre_z) ** 2
    )
    kernel = 1.0 / (1.0 + distance / float(RADIUS * RADIUS))
    return jnp.where(pair_live, kernel, 0.0).astype(jnp.bfloat16)


def spectral_filter(lifted_grid, spectral_weight):
    grid_tables = mode_tables(G, M)
    columns = lax.all_to_all(lifted_grid, "slab", split_axis=1, concat_axis=0, tiled=True)
    real_part, imag_part = forward(columns.astype(jnp.float32), None, 0, grid_tables)
    real_part, imag_part = forward(real_part, imag_part, 2, grid_tables)
    real_part, imag_part = (
        lax.all_to_all(
            real_part.astype(jnp.bfloat16), "slab", split_axis=2, concat_axis=1, tiled=True
        ).astype(real_part.dtype),
        lax.all_to_all(
            imag_part.astype(jnp.bfloat16), "slab", split_axis=2, concat_axis=1, tiled=True
        ).astype(imag_part.dtype),
    )
    real_part, imag_part = forward(real_part, imag_part, 1, grid_tables)
    real_part, imag_part = mix_modes(real_part, imag_part, spectral_weight)
    real_part, imag_part = inverse(real_part, imag_part, 1, grid_tables, G, True)
    real_part, imag_part = (
        lax.all_to_all(
            real_part.astype(jnp.bfloat16), "slab", split_axis=1, concat_axis=2, tiled=True
        ).astype(real_part.dtype),
        lax.all_to_all(
            imag_part.astype(jnp.bfloat16), "slab", split_axis=1, concat_axis=2, tiled=True
        ).astype(imag_part.dtype),
    )
    real_part, imag_part = inverse(real_part, imag_part, 2, grid_tables, G, True)
    spatial = inverse(real_part, imag_part, 0, grid_tables, G, False)
    return lax.all_to_all(
        spatial.astype(jnp.bfloat16), "slab", split_axis=0, concat_axis=1, tiled=True
    ).astype(spatial.dtype)


def shards(
    point_feat,
    point_pos,
    pair_point,
    pair_cell,
    lift_weight,
    spectral_weight,
    skip_weight,
    proj_weight,
):
    slab_count = lax.axis_size("slab")
    planes = G // slab_count
    slab_cells = planes * G * G
    pair_live = pair_cell[0] >= 0
    point_ids = jnp.maximum(pair_point[0], 0)
    cell_ids = jnp.maximum(pair_cell[0], 0)
    slab_first = (jnp.arange(slab_count) * planes)[:, None]
    positions = point_pos[:, point_ids]
    weights = pair_weights(positions, cell_ids, slab_first, pair_live)
    features = point_feat[point_ids]
    got_feat, got_weight, got_cells = (
        lax.all_to_all(features, "slab", split_axis=0, concat_axis=0, tiled=True),
        lax.all_to_all(weights, "slab", split_axis=0, concat_axis=0, tiled=True),
        lax.all_to_all(cell_ids, "slab", split_axis=0, concat_axis=0, tiled=True),
    )
    flat_cells = got_cells.reshape(-1)
    got_float = got_weight.astype(jnp.float32).reshape(-1)
    terms = got_float[:, None] * got_feat.reshape(-1, C).astype(jnp.float32)
    cell_sum = jax.ops.segment_sum(terms, flat_cells, num_segments=slab_cells)
    weight_sum = jax.ops.segment_sum(got_float, flat_cells, num_segments=slab_cells)
    normalized = (cell_sum / (1.0 + weight_sum)[:, None]).astype(jnp.bfloat16)
    lifted = jnp.dot(normalized, lift_weight, preferred_element_type=jnp.float32).astype(
        jnp.bfloat16
    )
    skip_part = jnp.dot(lifted, skip_weight, preferred_element_type=jnp.float32)
    spectral_part = spectral_filter(lifted.reshape(planes, G, G, C), spectral_weight)
    hidden = jax.nn.gelu(spectral_part.reshape(-1, C) + skip_part).astype(jnp.bfloat16)
    cell_rows = hidden[flat_cells].reshape(slab_count, -1, C)
    returned = lax.all_to_all(cell_rows, "slab", split_axis=0, concat_axis=0, tiled=True)
    own_float = weights.astype(jnp.float32).reshape(-1)
    flat_points = point_ids.reshape(-1)
    point_terms = own_float[:, None] * returned.reshape(-1, C).astype(jnp.float32)
    point_sum = jax.ops.segment_sum(point_terms, flat_points, num_segments=point_feat.shape[0])
    point_weight = jax.ops.segment_sum(own_float, flat_points, num_segments=point_feat.shape[0])
    point_mean = (point_sum / (1.0 + point_weight)[:, None]).astype(jnp.bfloat16)
    return jnp.dot(point_mean, proj_weight, preferred_element_type=jnp.float32).astype(jnp.bfloat16)


def solution(mesh):
    in_specs = (
        P(("groups", "slab"), None),
        P(None, ("groups", "slab")),
        P(("groups", "slab"), None, None),
        P(("groups", "slab"), None, None),
        P(),
        P(None, None, "slab", None, None, None),
        P(),
        P(),
    )
    out_specs = P(("groups", "slab"), None)
    return jax.shard_map(shards, mesh=mesh, in_specs=in_specs, out_specs=out_specs, check_vma=False)
```

profile of v0, /device:TPU:0, one launch (start us, length us, event | category | flops | bytes accessed | tf_op | source)
XLA Modules:
  0.0 2181.5 jit_solution(16815173783752454783)
XLA Ops:
  2.5 10.8 gather_fusion
  17.0 7.4 all-to-all-start.1
  26.4 4.4 all-to-all-done.1
  30.8 3.5 all-to-all-start
  35.5 12.1 gather_fusion.1
  48.8 6.0 all-to-all-start.2
  54.8 28.8 %scatter_custom_fusion.1 = f32[131072]{0:T(1024)} fusion(s32[4096]{0:T(1024)S(1)} %bitcast.260, f32[4096]{0:T(1024)S(1)} %bitcast.263, f32[]{:T(128)} %constant.94.clone.1), kind=kCustom, calls=%fused_computation.97 | custom fusion | flops 4096 | bytes 524292 | tf_op jit(solution)/shard_map/scatter-add | solution.py:132
  84.6 21.1 broadcast_in_dim.28
  105.6 516.7 %scatter_fusion = f32[131072,64]{1,0:T(8,128)} fusion(f32[131072,64]{1,0:T(8,128)} %broadcast_in_dim.28, s32[4096]{0:T(1024)S(1)} %bitcast.261, f32[4096,64]{1,0:T(8,128)S(1)} %copy.116), kind=kCustom, calls=%fused_computation.3 | custom fusion | flops 262144 | bytes 3162112 | tf_op jit(solution)/shard_map/scatter-add | solution.py:131
  622.4 58.3 %convolution_convert_fusion = bf16[131072,64]{0,1:T(8,128)(2,1)S(1)} fusion(bf16[64,64]{1,0:T(8,128)(2,1)S(1)} %copy-done, f32[131072,64]{1,0:T(8,128)} %scatter_fusion, f32[131072]{0:T(1024)S(1)} %copy-done.9), kind=kOutput, calls=%fused_computation.8 | convolution fusion | flops 1098907648 | bytes 50864128 | tf_op jit(solution)/shard_map/dot_general | solution.py:134
  680.7 5.9 copy.167
  686.9 36.1 %copy.117 = bf16[8,128,128,64]{2,0,3,1:T(8,128)(2,1)} copy(bf16[8,128,128,64]{2,1,0,3:T(8,128)(2,1)S(1)} %bitcast.231) | data formatting | bytes 33554432 | tf_op jit(solution)/shard_map/reshape | solution.py:138
  723.0 7.5 all-to-all-start.3
  730.5 296.7 %all-to-all-done.3 = bf16[8,128,128,64]{2,0,3,1:T(8,128)(2,1)} async-done(((bf16[8,128,128,64]{2,0,3,1:T(8,128)(2,1)}), bf16[8,128,128,64]{2,0,3,1:T(8,128)(2,1)}, u32[]{:S(2)}, u32[]{:S(2)}) %all-to-all-start.3) | async-done | bytes 16777248 | tf_op jit(solution)/shard_map/all_to_all | solution.py:74
  1027.3 10.3 fusion.31
  1037.6 13.3 fusion.10
  1051.0 26.9 %fusion.23 = f32[32,32,8,64]{3,0,2,1:T(8,128)S(1)} fusion(f32[32,8,128,64]{2,0,3,1:T(8,128)S(1)} %fusion.31, f32[128]{0:T(128)S(1)} %iota_convert_fusion, f32[32]{0:T(128)S(1)} %fusion.241), kind=kOutput, calls=%fused_computation.35 | convolution fusion | flops 805314560 | bytes 10486400 | tf_op jit(solution)/shard_map/dot_general | solution.py:21
  1077.9 26.9 %fusion.54 = bf16[32,8,32,64]{3,2,1,0:T(8,128)(2,1)S(1)} fusion(f32[32,32,8,64]{3,0,2,1:T(8,128)S(1)} %fusion.23, f32[32,8,128,64]{2,0,3,1:T(8,128)S(1)} %fusion.10, f32[128]{0:T(128)S(1)} %iota_convert_fusion, f32[32]{0:T(128)S(1)} %fusion.241), kind=kOutput, calls=%fused_computation.67 | convolution fusion | flops 806363136 | bytes 11534976 | tf_op jit(solution)/shard_map/dot_general | solution.py:21
  1105.6 2.5 reshape.507
  1108.1 70.2 %all-to-all-start.4 = ((bf16[16,2,16384]{2,1,0:T(2,128)(2,1)}), bf16[16,2,16384]{2,1,0:T(2,128)(2,1)S(1)}, u32[]{:S(2)}, u32[]{:S(2)}) async-start(bf16[16,2,16384]{2,1,0:T(2,128)(2,1)} %reshape.507), calls=%async_computation.4 | async-start | bytes 2097152 | tf_op jit(solution)/shard_map/all_to_all | solution.py:78
  1178.3 25.8 %fusion.21 = f32[32,32,8,64]{3,0,2,1:T(8,128)S(1)} fusion(f32[32,8,128,64]{2,0,3,1:T(8,128)} %copy-done.3, f32[128]{0:T(128)S(1)} %iota_convert_fusion, f32[32]{0:T(128)S(1)} %fusion.241), kind=kOutput, calls=%fused_computation.33 | convolution fusion | flops 805314560 | bytes 10486400 | tf_op jit(solution)/shard_map/dot_general | solution.py:21
  1204.1 26.2 %fusion.57 = bf16[32,8,32,64]{3,2,1,0:T(8,128)(2,1)S(1)} fusion(f32[32,32,8,64]{3,0,2,1:T(8,128)S(1)} %fusion.21, f32[32,8,128,64]{2,0,3,1:T(8,128)} %copy-done.2, f32[128]{0:T(128)S(1)} %iota_convert_fusion, f32[32]{0:T(128)S(1)} %fusion.241), kind=kOutput, calls=%fused_computation.68 | convolution fusion | flops 806363136 | bytes 11534976 | tf_op jit(solution)/shard_map/dot_general | solution.py:21
  1231.1 2.3 reshape.509
  1233.4 6.2 all-to-all-start.5
  1239.6 1.3 reshape.508
  1241.0 2.1 fusion.38
  1244.1 18.5 all-to-all-done.5
  1262.6 3.8 reshape.510
  1266.4 2.3 fusion.68
  1270.1 26.1 %fusion.46 = f32[32,32,2,1,64,1]{4,3,5,2,1,0:T(1,128)S(1)} fusion(bf16[32,32,2,2,64,64]{5,4,3,2,1,0:T(8,128)(2,1)} %param.13, bf16[32,32,2,2,64,1]{4,1,2,0,3,5:T(8,128)(2,1)S(1)} %get-tuple-element.7), kind=kOutput, calls=%fused_computation.55 | convolution fusion | flops 33554432 | bytes 34603008 | tf_op jit(solution)/shard_map/abcsd,abcsde->abce/dot_general | solution.py:55
  1296.3 3.5 fusion.77
  1299.7 25.9 %fusion.48 = f32[32,32,2,1,64,1]{4,3,5,2,1,0:T(1,128)S(1)} fusion(bf16[32,32,2,2,64,64]{5,4,3,2,1,0:T(8,128)(2,1)} %param.13, bf16[32,32,2,2,64,1]{4,1,2,0,3,5:T(8,128)(2,1)S(1)} %get-tuple-element.8), kind=kOutput, calls=%fused_computation.57 | convolution fusion | flops 33554432 | bytes 34603008 | tf_op jit(solution)/shard_map/abcsd,abcsde->abce/dot_general | solution.py:54
  1326.6 3.5 fusion.61
  1330.1 2.9 copy.135
  1333.1 2.3 reshape.513
  1335.3 7.3 all-to-all-start.7
  1342.7 4.7 fusion.81
  1347.4 4.7 fusion.60
  1352.1 2.9 copy.131
  1355.1 2.3 reshape.511
  1357.4 8.3 all-to-all-done.7
  1365.6 7.0 all-to-all-start.6
  1372.7 5.0 reshape.514
  1377.7 2.4 copy.246
  1380.5 4.1 copy.138
  1384.7 7.7 fusion.133
  1392.4 5.9 fusion.142
  1398.3 1.5 reshape.512
  1399.9 2.4 copy.247
  1402.7 4.1 copy.134
  1406.8 7.5 fusion.146
  1414.4 6.0 fusion.131
  1420.5 30.9 %fusion.15 = f32[128,8,128,64]{2,0,3,1:T(8,128)} fusion(f32[128,32,8,64]{0,1,3,2:T(8,128)S(1)} %fusion.146, f32[128,32,8,64]{0,1,3,2:T(8,128)S(1)} %bitcast.233, f32[128]{0:T(128)S(1)} %iota_convert_fusion, f32[32]{0:T(128)S(1)} %fusion.241), kind=kOutput, calls=%fused_computation.27 | convolution fusion | flops 3225427968 | bytes 50332288 | tf_op jit(solution)/shard_map/dot_general | solution.py:21
  1451.4 35.8 %multiply_convert_fusion = bf16[128,8,128,64]{2,0,3,1:T(8,128)(2,1)} fusion(f32[128,8,128,64]{2,0,3,1:T(8,128)} %fusion.15, f32[128,32,8,64]{0,1,3,2:T(8,128)S(1)} %bitcast.235, f32[128,32,8,64]{0,1,3,2:T(8,128)} %fusion.131, f32[128]{0:T(128)S(1)} %iota_convert_fusion, f32[32]{0:T(128)S(1)} %fusion.241), kind=kOutput, calls=%fused_computation.19 | convolution fusion | flops 3250593792 | bytes 67109504 | tf_op jit(solution)/shard_map/dot_general | solution.py:21
  1487.2 16.8 copy.141
  1504.0 6.3 all-to-all-start.8
  1510.3 296.7 %all-to-all-done.8 = bf16[128,8,128,64]{2,3,1,0:T(8,128)(2,1)} async-done(((bf16[128,8,128,64]{2,3,1,0:T(8,128)(2,1)}), bf16[128,8,128,64]{2,3,1,0:T(8,128)(2,1)}, u32[]{:S(2)}, u32[]{:S(2)}) %all-to-all-start.8) | async-done | bytes 16777248 | tf_op jit(solution)/shard_map/all_to_all | solution.py:98
  1807.0 19.1 copy.142
  1826.1 45.7 %fusion.7 = bf16[131072,64]{0,1:T(8,128)(2,1)} fusion(bf16[131072,64]{0,1:T(8,128)(2,1)} %copy-done.6, bf16[64,64]{1,0:T(8,128)(2,1)S(1)} %copy-done.22, f32[8,8,1024,128]{3,2,1,0:T(8,128)} %bitcast.236), kind=kOutput, calls=%fused_computation.18 | convolution fusion | flops 1157627904 | bytes 67117056 | tf_op jit(solution)/shard_map/dot_general | solution.py:137
  1871.8 30.0 %copy.143 = bf16[131072,64]{1,0:T(8,128)(2,1)} copy(bf16[131072,64]{0,1:T(8,128)(2,1)} %fusion.7) | data formatting | bytes 33554432 | tf_op jit(solution)/shard_map/convert_element_type | solution.py:139
  1901.9 149.0 %gather_fusion.2 = bf16[4096,64]{1,0:T(8,128)(2,1)S(1)} fusion(bf16[131072,64]{1,0:T(8,128)(2,1)} %copy.143, s32[4096]{0:T(1024)S(1)} %broadcast_clamp_fusion), kind=kCustom, calls=%fused_computation.2 | custom fusion | bytes 1064960 | tf_op jit(solution)/shard_map/gather | solution.py:140
  2052.0 71.7 %all-to-all-start.9 = ((bf16[16,256,64]{1,2,0:T(8,128)(2,1)}), bf16[16,256,64]{1,2,0:T(8,128)(2,1)S(1)}, u32[]{:S(2)}, u32[]{:S(2)}) async-start(bf16[16,256,64]{1,2,0:T(8,128)(2,1)} %copy.144), calls=%async_computation.9 | async-start | bytes 1048576 | tf_op jit(solution)/shard_map/all_to_all | solution.py:141
  2124.0 27.4 %scatter_custom_fusion.3 = f32[2048]{0:T(1024)S(1)} fusion(s32[4096]{0:T(1024)} %bitcast.273, f32[4096]{0:T(1024)S(1)} %fusion.238, f32[]{:T(128)} %constant.94.clone.1), kind=kCustom, calls=%fused_computation.259 | custom fusion | flops 4096 | bytes 8704 | tf_op jit(solution)/shard_map/scatter-add | solution.py:146
  2152.3 27.7 %scatter_custom_fusion.2 = f32[2048,64]{1,0:T(8,128)S(1)} fusion(s32[4096]{0:T(1024)} %bitcast.274, f32[4096,64]{1,0:T(8,128)S(1)} %copy.146, f32[]{:T(128)} %constant.92.clone.1), kind=kCustom, calls=%fused_computation.95 | custom fusion | flops 262144 | bytes 524800 | tf_op jit(solution)/shard_map/scatter-add | solution.py:145
  (115 shorter events, 21.3 us)
Async XLA Ops:
  0.0 622.4 %copy-start = (bf16[64,64]{1,0:T(8,128)(2,1)S(1)}, bf16[64,64]{1,0:T(8,128)(2,1)}, u32[]{:S(2)}) copy-start(bf16[64,64]{1,0:T(8,128)(2,1)} %param.12) | copy-start | bytes 24580
  0.0 30.8 %copy-start.20 = (s32[16]{0:T(128)}, s32[16]{0:T(128)S(1)}, u32[]{:S(2)}) copy-start(s32[16]{0:T(128)S(1)} %iota_multiply_fusion) | copy-start | bytes 196
  0.8 0.6 copy-start.18
  13.9 70.0 %copy-start.10 = (f32[16,256,3]{1,0,2:T(8,128)}, f32[16,256,3]{1,0,2:T(8,128)S(1)}, u32[]{:S(2)}) copy-start(f32[16,256,3]{1,0,2:T(8,128)S(1)} %copy.110) | copy-start | bytes 147460
  17.0 13.8 all-to-all-start.1
  30.8 18.0 all-to-all-start
  48.8 56.9 %copy-start.12 = (s32[16,1,256]{2,1,0:T(1,128)}, s32[16,1,256]{2,1,0:T(1,128)S(1)}, u32[]{:S(2)}) copy-start(s32[16,1,256]{2,1,0:T(1,128)S(1)} %all-to-all-done) | copy-start | bytes 49156
  48.8 34.9 %all-to-all-start.2 = ((bf16[16,256,64]{1,2,0:T(8,128)(2,1)}), bf16[16,256,64]{1,2,0:T(8,128)(2,1)S(1)}, u32[]{:S(2)}, u32[]{:S(2)}) async-start(bf16[16,256,64]{1,2,0:T(8,128)(2,1)} %copy.114), calls=%async_computation.2 | async-start | bytes 1048576 | tf_op jit(solution)/shard_map/all_to_all | solution.py:124
  105.6 516.7 %copy-start.9 = (f32[131072]{0:T(1024)S(1)}, f32[131072]{0:T(1024)}, u32[]{:S(2)}) copy-start(f32[131072]{0:T(1024)} %scatter_custom_fusion.1) | copy-start | bytes 1572868
  680.7 6.2 copy-start.6
  723.0 304.3 %all-to-all-start.3 = ((bf16[8,128,128,64]{2,0,3,1:T(8,128)(2,1)}), bf16[8,128,128,64]{2,0,3,1:T(8,128)(2,1)}, u32[]{:S(2)}, u32[]{:S(2)}) async-start(bf16[8,128,128,64]{2,0,3,1:T(8,128)(2,1)} %copy.117), calls=%async_computation.3 | async-start | bytes 33554432 | tf_op jit(solution)/shard_map/all_to_all | solution.py:74
  1037.6 13.4 copy-start.3
  1051.0 53.8 %copy-start.2 = (f32[32,8,128,64]{2,0,3,1:T(8,128)}, f32[32,8,128,64]{2,0,3,1:T(8,128)S(1)}, u32[]{:S(2)}) copy-start(f32[32,8,128,64]{2,0,3,1:T(8,128)S(1)} %fusion.10) | copy-start | bytes 25165828
  1108.1 125.3 %all-to-all-start.4 = ((bf16[16,2,16384]{2,1,0:T(2,128)(2,1)}), bf16[16,2,16384]{2,1,0:T(2,128)(2,1)S(1)}, u32[]{:S(2)}, u32[]{:S(2)}) async-start(bf16[16,2,16384]{2,1,0:T(2,128)(2,1)} %reshape.507), calls=%async_computation.4 | async-start | bytes 2097152 | tf_op jit(solution)/shard_map/all_to_all | solution.py:78
  1233.4 29.2 %all-to-all-start.5 = ((bf16[16,2,16384]{2,1,0:T(2,128)(2,1)}), bf16[16,2,16384]{2,1,0:T(2,128)(2,1)}, u32[]{:S(2)}, u32[]{:S(2)}) async-start(bf16[16,2,16384]{2,1,0:T(2,128)(2,1)} %reshape.509), calls=%async_computation.5 | async-start | bytes 2097152 | tf_op jit(solution)/shard_map/all_to_all | solution.py:81
  1296.2 29.4 %copy-start.7 = (f32[32,32,2,1,64,1]{4,3,5,2,1,0:T(1,128)}, f32[32,32,2,1,64,1]{4,3,5,2,1,0:T(1,128)S(1)}, u32[]{:S(2)}) copy-start(f32[32,32,2,1,64,1]{4,3,5,2,1,0:T(1,128)S(1)} %fusion.46) | copy-start | bytes 1572868
  1325.6 1.0 copy-start.8
  1335.3 30.3 %all-to-all-start.7 = ((bf16[16,2,16384]{2,1,0:T(2,128)(2,1)}), bf16[16,2,16384]{2,1,0:T(2,128)(2,1)}, u32[]{:S(2)}, u32[]{:S(2)}) async-start(bf16[16,2,16384]{2,1,0:T(2,128)(2,1)} %reshape.513), calls=%async_computation.7 | async-start | bytes 2097152 | tf_op jit(solution)/shard_map/all_to_all | solution.py:92
  1365.6 32.7 %all-to-all-start.6 = ((bf16[16,2,16384]{2,1,0:T(2,128)(2,1)}), bf16[16,2,16384]{2,1,0:T(2,128)(2,1)S(1)}, u32[]{:S(2)}, u32[]{:S(2)}) async-start(bf16[16,2,16384]{2,1,0:T(2,128)(2,1)} %reshape.511), calls=%async_computation.6 | async-start | bytes 2097152 | tf_op jit(solution)/shard_map/all_to_all | solution.py:89
  1384.7 7.7 copy-start.4
  1406.8 7.6 copy-start.5
  1406.8 13.6 slice-start
  1414.4 6.1 slice-start.1
  1414.4 37.0 %slice-start.2 = ((s8[8388608]{0:T(1024)(128)(4,1)}), s8[4194304]{0:T(1024)(128)(4,1)S(1)}, s32[]{:S(2)}) async-start(s8[8388608]{0:T(1024)(128)(4,1)} %bitcast.234), calls=%async_computation.12 | async-start | bytes 8388608
  1420.5 31.0 %slice-start.3 = ((s8[8388608]{0:T(1024)(128)(4,1)}), s8[4194304]{0:T(1024)(128)(4,1)S(1)}, s32[]{:S(2)}) async-start(s8[8388608]{0:T(1024)(128)(4,1)} %bitcast.234), calls=%async_computation.13 | async-start | bytes 8388608
  1504.0 6.3 copy-start.13
  1504.0 303.0 %all-to-all-start.8 = ((bf16[128,8,128,64]{2,3,1,0:T(8,128)(2,1)}), bf16[128,8,128,64]{2,3,1,0:T(8,128)(2,1)}, u32[]{:S(2)}, u32[]{:S(2)}) async-start(bf16[128,8,128,64]{2,3,1,0:T(8,128)(2,1)} %copy.141), calls=%async_computation.8 | async-start | bytes 33554432 | tf_op jit(solution)/shard_map/all_to_all | solution.py:98
  1807.0 19.1 copy-start.22
  1901.8 221.8 %copy-start.11 = (f32[16,256,3]{1,0,2:T(8,128)S(1)}, f32[16,256,3]{1,0,2:T(8,128)}, u32[]{:S(2)}) copy-start(f32[16,256,3]{1,0,2:T(8,128)} %copy-done.10) | copy-start | bytes 147460
  1901.8 221.9 %copy-start.19 = (pred[1,16,256]{2,1,0:T(8,128)(4,1)S(1)}, pred[1,16,256]{2,1,0:T(8,128)(4,1)}, u32[]{:S(2)}) copy-start(pred[1,16,256]{2,1,0:T(8,128)(4,1)} %get-tuple-element.6) | copy-start | bytes 12292
  1901.8 221.9 %copy-start.17 = (s32[2,2,8,128]{3,2,1,0:T(8,128)S(1)}, s32[2,2,8,128]{3,2,1,0:T(8,128)}, u32[]{:S(2)}) copy-start(s32[2,2,8,128]{3,2,1,0:T(8,128)} %get-tuple-element.14) | copy-start | bytes 49156
  1901.8 222.0 %copy-start.16 = (s32[2,2,8,128]{3,2,1,0:T(8,128)S(1)}, s32[2,2,8,128]{3,2,1,0:T(8,128)}, u32[]{:S(2)}) copy-start(s32[2,2,8,128]{3,2,1,0:T(8,128)} %get-tuple-element.15) | copy-start | bytes 49156
  1901.8 222.0 %copy-start.15 = (s32[2,2,8,128]{3,2,1,0:T(8,128)S(1)}, s32[2,2,8,128]{3,2,1,0:T(8,128)}, u32[]{:S(2)}) copy-start(s32[2,2,8,128]{3,2,1,0:T(8,128)} %get-tuple-element.16) | copy-start | bytes 49156
  1901.8 222.0 %copy-start.21 = (s32[16]{0:T(128)S(1)}, s32[16]{0:T(128)}, u32[]{:S(2)}) copy-start(s32[16]{0:T(128)} %copy-done.20) | copy-start | bytes 196
  1901.8 222.1 %copy-start.14 = (s32[1,16,256]{2,1,0:T(8,128)S(1)}, s32[1,16,256]{2,1,0:T(8,128)}, u32[]{:S(2)}) copy-start(s32[1,16,256]{2,1,0:T(8,128)} %param.11) | copy-start | bytes 49156
  1901.9 279.4 %copy-start.1 = (bf16[64,64]{1,0:T(8,128)(2,1)S(1)}, bf16[64,64]{1,0:T(8,128)(2,1)}, u32[]{:S(2)}) copy-start(bf16[64,64]{1,0:T(8,128)(2,1)} %param.12) | copy-start | bytes 24580
  2050.8 129.1 %copy-start.23 = (bf16[64,64]{1,0:T(8,128)(2,1)S(1)}, bf16[64,64]{1,0:T(8,128)(2,1)}, u32[]{:S(2)}) copy-start(bf16[64,64]{1,0:T(8,128)(2,1)} %param.15) | copy-start | bytes 24580
  2052.0 99.5 %all-to-all-start.9 = ((bf16[16,256,64]{1,2,0:T(8,128)(2,1)}), bf16[16,256,64]{1,2,0:T(8,128)(2,1)S(1)}, u32[]{:S(2)}, u32[]{:S(2)}) async-start(bf16[16,256,64]{1,2,0:T(8,128)(2,1)} %copy.144), calls=%async_computation.9 | async-start | bytes 1048576 | tf_op jit(solution)/shard_map/all_to_all | solution.py:141
where the time goes:
time: 2200 us; the launch traced here: 2180 us
  waiting for transfers between devices  625 us (28%)
  other arithmetic  605 us (28%)
  matrix products  404 us (18%)
  local copies, waits for them, and re-layouts  354 us (16%)
  starting transfers between devices  193 us (9%)
    scatter-add x1, other arithmetic, shards(): cell_sum = jax.ops.segment_sum(terms, flat_cells, num_segments=slab_cells)  517 us
    all_to_all x1, waiting for transfers between devices, spectral_filter(): lax.all_to_all(lifted_grid, 'slab', split_axis=1, concat_axis=0, tiled=True)  297 us
    all_to_all x1, waiting for transfers between devices, spectral_filter(): lax.all_to_all(spatial.astype(jnp.bfloat16), 'slab', split_axis=0, concat...  297 us
    dot_general x20, matrix products, along(): jnp.tensordot(table, tensor, axes=((table_axis,), (dimension,)), precisio...  246 us
    gather x1, local copies, waits for them, and re-layouts, shards(): cell_rows = hidden[flat_cells].reshape(slab_count, -1, C)  149 us
    all_to_all x1, starting transfers between devices, shards(): lax.all_to_all(cell_rows, 'slab', split_axis=0, concat_axis=0, tiled=True)  71.7 us
    all_to_all x1, starting transfers between devices, spectral_filter(): lax.all_to_all(real_part.astype(jnp.bfloat16), 'slab', split_axis=2, conc...  70.2 us
    dot_general x1, matrix products, shards(): jnp.dot(normalized, lift_weight, preferred_element_type=jnp.float32)  58.3 us
  transfers between devices with their start and end apart: 10, of which 5 were waited for; matrix products, arithmetic and copies ran while one was open for 8% of the time, Pallas kernels for 0%

commit v1 on v0

v1 whole, which is shorter than its diff:
```python
import functools

import jax
import jax.numpy as jnp
from jax import lax
from jax.experimental import pallas as pl
from jax.experimental.pallas import tpu as pltpu
from jax.sharding import PartitionSpec as P

G = 128
C = 64
M = 32
RADIUS = 2
LISTS = 5
CAP = 256
VMEM_LIMIT = 48 * 1024 * 1024
F32 = jnp.float32
BF16 = jnp.bfloat16


def params():
    return pltpu.CompilerParams(vmem_limit_bytes=VMEM_LIMIT)


def frequencies(count, first=0):
    k = first + jnp.arange(count)
    return jnp.where(k < M // 2, k, k - M)


def waves(frequency, length):
    phase = (frequency[:, None] * jnp.arange(length)[None, :]) % length
    angle = (2.0 * jnp.pi / length) * phase.astype(F32)
    return jnp.cos(angle), jnp.sin(angle)


def nt_dot(left, right):
    return lax.dot_general(left, right, (((1,), (1,)), ((), ())), preferred_element_type=F32)


def dot(left, right):
    return jnp.dot(left, right, preferred_element_type=F32)


def prep_kernel(feat_ref, pos_ref, point_ref, cell_ref, slab_ref, lift_ref, lifted_ref, meta_ref, planes):
    points = feat_ref.shape[1]
    pos = pos_ref[...]
    high = pos.astype(BF16)
    rest = pos - high.astype(F32)
    middle = rest.astype(BF16)
    low = (rest - middle.astype(F32)).astype(BF16)
    lift = lift_ref[...]
    feat = feat_ref[...]
    for k in range(LISTS):
        place = pl.ds(k * CAP, CAP)
        point = point_ref[k : k + 1, :]
        cell = cell_ref[k : k + 1, :]
        live = cell >= 0
        cell = jnp.maximum(cell, 0)
        rows = lax.broadcasted_iota(jnp.int32, (points, CAP), 0)
        hot = jnp.where(rows == point, 1.0, 0.0).astype(BF16)
        got = dot(feat, hot).astype(BF16)
        lifted_ref[:, place] = lax.dot_general(
            lift, got, (((0,), (0,)), ((), ())), preferred_element_type=F32
        ).astype(BF16)
        at = dot(high, hot) + dot(middle, hot) + dot(low, hot)
        x = cell // (G * G) + slab_ref[k : k + 1, :] * planes
        y = cell // G % G
        z = cell % G
        xf, yf, zf = x.astype(F32), y.astype(F32), z.astype(F32)
        distance = (
            (at[0:1] - (xf + 0.5)) ** 2 + (at[1:2] - (yf + 0.5)) ** 2 + (at[2:3] - (zf + 0.5)) ** 2
        )
        kernel = 1.0 / (1.0 + distance / float(RADIUS * RADIUS))
        weight = jnp.where(live, kernel, 0.0)
        meta_ref[:, place] = jnp.concatenate(
            [xf, yf, zf, weight, jnp.zeros((12, CAP), F32)], axis=0
        ).astype(BF16)


def share_kernel(slab_ref, key_ref, weight_ref, share_ref, bucket, count):
    lists = key_ref.shape[0]
    slabs = count.shape[0]

    def clear(s, _):
        count[s] = 0
        return 0

    lax.fori_loop(0, slabs, clear, 0)

    def fill(i, _):
        s = slab_ref[i]
        n = count[s]
        bucket[s * lists + n] = i
        count[s] = n + 1
        return 0

    lax.fori_loop(0, lists, fill, 0)
    share_ref[...] = jnp.zeros_like(share_ref)

    def per_slab(s, _):
        n = count[s]

        def per_source(q, _):
            j = bucket[s * lists + q]
            both = jnp.concatenate([key_ref[j], weight_ref[j], jnp.zeros((6, CAP), F32)], axis=0)
            turned = both.T
            key = turned[:, 0:1]
            weight = turned[:, 1:2]

            def per_target(p, _):
                i = bucket[s * lists + p]
                terms = jnp.where(key == key_ref[i], weight, 0.0)
                share_ref[i] += jnp.sum(terms, axis=0, keepdims=True)
                return 0

            return lax.fori_loop(0, n, per_target, 0)

        return lax.fori_loop(0, n, per_source, 0)

    lax.fori_loop(0, slabs, per_slab, 0)
    share_ref[...] = weight_ref[...] / (1.0 + share_ref[...])


def forward_kernel(slab_ref, lifted_ref, meta_ref, share_ref, tab_y_ref, tab_z_ref, planes_ref, wave_ref, total, planes):
    region = pl.program_id(0)
    rows = wave_ref.shape[1]

    @pl.when(region == 0)
    def _():
        total[...] = jnp.zeros_like(total)

    for k in range(LISTS):
        place = pl.ds(k * CAP, CAP)
        slab = slab_ref[region * LISTS + k]
        meta = meta_ref[0, :, place].astype(F32)
        line = lax.broadcasted_iota(jnp.int32, (G, CAP), 0).astype(F32)
        hot_y = jnp.where(line == meta[1:2], 1.0, 0.0).astype(BF16)
        hot_z = jnp.where(line == meta[2:3], 1.0, 0.0).astype(BF16)
        along_y = dot(tab_y_ref[...], hot_y)
        along_z = dot(tab_z_ref[...], hot_z)
        wave = along_y[:rows] * along_z[:rows] + along_y[rows:] * along_z[rows:]
        wave = wave.astype(BF16)
        wave_ref[0, :, place] = wave
        scaled = (lifted_ref[0, :, place].astype(F32) * share_ref[k]).astype(BF16)
        local = meta[0:1] - (slab * planes).astype(F32)
        parts = [
            scaled * jnp.where(local == float(p), 1.0, 0.0).astype(BF16) for p in range(planes)
        ]
        total[slab] += nt_dot(jnp.concatenate(parts, axis=0), wave)

    @pl.when(region == pl.num_programs(0) - 1)
    def _():
        planes_ref[...] = total[...].astype(BF16)


def mix_kernel(coefficient_ref, weight_ref, out_ref):
    columns, depth = weight_ref.shape[1], coefficient_ref.shape[-1]
    for b in range(columns):
        weights = weight_ref[0, b].reshape(depth, C)
        out_ref[0, b] = dot(coefficient_ref[0, b], weights)


def inverse_kernel(slab_ref, meta_ref, wave_ref, field_ref, out_ref, planes):
    region = pl.program_id(0)
    for k in range(LISTS):
        place = pl.ds(k * CAP, CAP)
        slab = slab_ref[region * LISTS + k]
        local = meta_ref[0, :, place].astype(F32)[0:1] - (slab * planes).astype(F32)
        values = dot(field_ref[slab], wave_ref[0, :, place])
        total = jnp.zeros((C, CAP), F32)
        for p in range(planes):
            total += jnp.where(local == float(p), values[p * C : (p + 1) * C], 0.0)
        out_ref[0, :, place] = total.astype(BF16)


def cell_kernel(slab_ref, own_slab_ref, lifted_ref, share_ref, key_ref, own_key_ref, out_ref):
    regions = lifted_ref.shape[0]
    for k in range(LISTS):
        place = pl.ds(k * CAP, CAP)
        out_ref[:, place] = jnp.zeros((C, CAP), F32)
        own = own_key_ref[k : k + 1, :]
        turned = jnp.broadcast_to(own, (8, CAP)).T[:, 0:1]
        slab = own_slab_ref[k]

        def per_region(r, _):
            for m in range(LISTS):

                @pl.when(slab_ref[r * LISTS + m] == slab)
                def _():
                    same = jnp.where(turned == key_ref[r * LISTS + m], 1.0, 0.0).astype(BF16)
                    terms = lifted_ref[r, :, pl.ds(m * CAP, CAP)].astype(F32) * share_ref[r * LISTS + m]
                    out_ref[:, place] += nt_dot(terms.astype(BF16), same)

            return 0

        lax.fori_loop(0, regions, per_region, 0)


def decode_kernel(spectral_ref, cell_ref, meta_ref, point_ref, skip_ref, proj_ref, out_ref):
    points = out_ref.shape[1]
    total = jnp.zeros((C + 16, points), F32)
    for k in range(LISTS):
        place = pl.ds(k * CAP, CAP)
        skip = lax.dot_general(
            skip_ref[...],
            cell_ref[:, place].astype(BF16),
            (((0,), (0,)), ((), ())),
            preferred_element_type=F32,
        )
        u = spectral_ref[:, place].astype(F32) + skip
        hidden = 0.5 * u * (1.0 + jnp.tanh(0.7978845608028654 * (u + 0.044715 * u * u * u)))
        hidden = jnp.concatenate([hidden, jnp.ones((16, CAP), F32)], axis=0).astype(BF16)
        weight = meta_ref[:, place].astype(F32)[3:4]
        rows = lax.broadcasted_iota(jnp.int32, (points, CAP), 0)
        hot = jnp.where(rows == point_ref[k : k + 1, :], weight, 0.0).astype(BF16)
        total += nt_dot(hidden, hot)
    mean = (total[:C] / (1.0 + total[C : C + 1])).astype(BF16)
    out_ref[...] = lax.dot_general(
        proj_ref[...], mean, (((0,), (0,)), ((), ())), preferred_element_type=F32
    ).astype(BF16)


def compact(lists, live):
    rank = jnp.cumsum(live.astype(jnp.int32)) - 1
    hot = live[None, :] & (rank[None, :] == jnp.arange(LISTS)[:, None])
    return jnp.sum(jnp.where(hot[:, :, None], lists[None] + 1, 0), axis=1) - 1, hot


def pad8(array):
    return jnp.concatenate([array, jnp.full((8 - LISTS, array.shape[1]), -1, array.dtype)], axis=0)


VMEM = pl.BlockSpec(memory_space=pltpu.VMEM)
SMEM = pl.BlockSpec(memory_space=pltpu.SMEM)


def shards(
    point_feat,
    point_pos,
    pair_point,
    pair_cell,
    lift_weight,
    spectral_weight,
    skip_weight,
    proj_weight,
):
    slabs = lax.axis_size("slab")
    me = lax.axis_index("slab")
    planes = G // slabs
    own_modes = spectral_weight.shape[2]
    rows = 2 * M * own_modes
    slots = LISTS * CAP
    lists = slabs * LISTS
    points = point_feat.shape[0]

    live = pair_cell[0, :, 0] >= 0
    cells, hot = compact(pair_cell[0], live)
    point_ids, _ = compact(pair_point[0], live)
    own_slab = jnp.sum(jnp.where(hot, jnp.arange(slabs)[None, :], 0), axis=1).astype(jnp.int32)
    cells, point_ids = pad8(cells), pad8(point_ids)
    slab_rows = jnp.broadcast_to(own_slab[:, None], (LISTS, CAP))

    lifted, meta = pl.pallas_call(
        functools.partial(prep_kernel, planes=planes),
        out_shape=(
            jax.ShapeDtypeStruct((C, slots), BF16),
            jax.ShapeDtypeStruct((16, slots), BF16),
        ),
        in_specs=[VMEM] * 6,
        out_specs=(VMEM, VMEM),
        compiler_params=params(),
        name="prep",
    )(point_feat.T, point_pos, point_ids, cells, pad8(slab_rows), lift_weight)

    all_meta = lax.all_gather(meta, "slab")
    all_lifted = lax.all_gather(lifted, "slab")

    def keys(values):
        values = values.astype(F32)
        return (values[..., 0, :] * G + values[..., 1, :]) * G + values[..., 2, :]

    key = keys(all_meta).reshape(lists, 1, CAP)
    weight = all_meta[:, 3].astype(F32).reshape(lists, 1, CAP)
    slab_ids = (all_meta[:, 0, ::CAP].astype(jnp.int32) // planes).reshape(lists)
    own_key = pad8(keys(meta).reshape(LISTS, CAP))

    share = pl.pallas_call(
        share_kernel,
        out_shape=jax.ShapeDtypeStruct((lists, 1, CAP), F32),
        in_specs=[SMEM, VMEM, VMEM],
        out_specs=VMEM,
        scratch_shapes=[
            pltpu.SMEM((slabs * lists,), jnp.int32),
            pltpu.SMEM((slabs,), jnp.int32),
        ],
        compiler_params=params(),
        name="share",
    )(slab_ids, key, weight)

    cos_y, sin_y = waves(frequencies(M), G)
    cos_z, sin_z = waves(frequencies(own_modes, me * own_modes), G)
    cos_b, sin_b = jnp.repeat(cos_y, own_modes, 0), jnp.repeat(sin_y, own_modes, 0)
    cos_c, sin_c = jnp.tile(cos_z, (2 * M, 1)), jnp.tile(sin_z, (2 * M, 1))
    tab_y = jnp.concatenate([cos_b, -sin_b, -sin_b, -cos_b], 0).astype(BF16)
    tab_z = jnp.concatenate([cos_c, sin_c], 0).astype(BF16)

    def region_block(height):
        return pl.BlockSpec((1, height, slots), lambda r, ids: (r, 0, 0))

    def whole(shape):
        return pl.BlockSpec(shape, lambda r, ids: (0,) * len(shape))

    plane_sums, wave = pl.pallas_call(
        functools.partial(forward_kernel, planes=planes),
        out_shape=(
            jax.ShapeDtypeStruct((slabs, planes * C, rows), BF16),
            jax.ShapeDtypeStruct((slabs, rows, slots), BF16),
        ),
        grid_spec=pltpu.PrefetchScalarGridSpec(
            num_scalar_prefetch=1,
            grid=(slabs,),
            in_specs=[
                region_block(C),
                region_block(16),
                pl.BlockSpec((LISTS, 1, CAP), lambda r, ids: (r, 0, 0)),
                whole((2 * rows, G)),
                whole((2 * rows, G)),
            ],
            out_specs=(whole((slabs, planes * C, rows)), region_block(rows)),
            scratch_shapes=[pltpu.VMEM((slabs, planes * C, rows), F32)],
        ),
        compiler_params=params(),
        name="forward",
    )(slab_ids, all_lifted, all_meta, share, tab_y, tab_z)

    real_row = jnp.stack([cos_y, sin_y], 1)
    imag_row = jnp.stack([-sin_y, cos_y], 1)
    analysis = jnp.stack(
        [jnp.stack([real_row, -imag_row]), jnp.stack([imag_row, real_row])]
    ).astype(BF16)
    plane_sums = plane_sums.reshape(G, C, 2, M, own_modes)
    coefficients = jnp.einsum(
        "wsarx,xdrbc->abcwsd", analysis, plane_sums, preferred_element_type=F32
    ).astype(BF16)
    same = jnp.eye(own_modes, dtype=BF16)
    coefficients = coefficients[:, :, :, :, None] * same[:, None, :, None, None]
    coefficients = coefficients.reshape(M, M, 2 * own_modes, own_modes * 2 * C)
    coefficients = jnp.pad(coefficients, ((0, 0), (0, 0), (0, 8 - 2 * own_modes), (0, 0)))

    filtered = pl.pallas_call(
        mix_kernel,
        out_shape=jax.ShapeDtypeStruct((M, M, 8, C), F32),
        grid=(M,),
        in_specs=[
            pl.BlockSpec((1, M, 8, own_modes * 2 * C), lambda a: (a, 0, 0, 0)),
            pl.BlockSpec((1, M, own_modes, 2, C, C), lambda a: (a, 0, 0, 0, 0, 0)),
        ],
        out_specs=pl.BlockSpec((1, M, 8, C), lambda a: (a, 0, 0, 0)),
        compiler_params=params(),
        name="mix",
    )(coefficients, spectral_weight)

    filtered = filtered[:, :, : 2 * own_modes].reshape(M, M, own_modes, 2, C).astype(BF16)
    synthesis = jnp.stack([jnp.stack([cos_y, -sin_y]), jnp.stack([sin_y, cos_y])])
    synthesis = (synthesis / float(G * G * G)).astype(BF16)
    field = jnp.einsum(
        "rwax,abcwe->xerbc", synthesis, filtered, preferred_element_type=F32
    ).astype(BF16)
    field = field.reshape(slabs, planes * C, rows)

    partial = pl.pallas_call(
        functools.partial(inverse_kernel, planes=planes),
        out_shape=jax.ShapeDtypeStruct((slabs, C, slots), BF16),
        grid_spec=pltpu.PrefetchScalarGridSpec(
            num_scalar_prefetch=1,
            grid=(slabs,),
            in_specs=[region_block(16), region_block(rows), whole((slabs, planes * C, rows))],
            out_specs=region_block(C),
        ),
        compiler_params=params(),
        name="inverse",
    )(slab_ids, all_meta, wave, field)
    spectral = lax.psum_scatter(partial, "slab", scatter_dimension=0, tiled=False)

    cell_lifted = pl.pallas_call(
        cell_kernel,
        out_shape=jax.ShapeDtypeStruct((C, slots), F32),
        in_specs=[SMEM, SMEM, VMEM, VMEM, VMEM, VMEM],
        out_specs=VMEM,
        compiler_params=params(),
        name="cells",
    )(slab_ids, own_slab, all_lifted, share, key, own_key)

    out = pl.pallas_call(
        decode_kernel,
        out_shape=jax.ShapeDtypeStruct((C, points), BF16),
        in_specs=[VMEM] * 6,
        out_specs=VMEM,
        compiler_params=params(),
        name="decode",
    )(spectral, cell_lifted, meta, point_ids, skip_weight, proj_weight)
    return out.T


def solution(mesh):
    in_specs = (
        P(("groups", "slab"), None),
        P(None, ("groups", "slab")),
        P(("groups", "slab"), None, None),
        P(("groups", "slab"), None, None),
        P(),
        P(None, None, "slab", None, None, None),
        P(),
        P(),
    )
    out_specs = P(("groups", "slab"), None)
    return jax.shard_map(shards, mesh=mesh, in_specs=in_specs, out_specs=out_specs, check_vma=False)
```

time: 2200 us -> 319 us (0.14)
  other arithmetic: 605 us -> 4.03 us
  waiting for transfers between devices: 625 us -> 50 us
  matrix products: 404 us -> 4.42 us
  local copies, waits for them, and re-layouts: 354 us -> 61.3 us
  starting transfers between devices: 193 us -> 0.04 us
  Pallas kernels: 0 us -> 159 us
  blocking collectives: 0 us -> 25.5 us
    all_to_all x10 -> x0, waiting for transfers between devices: 625 us -> none  [the longest x1 297 us: spectral_filter(): lax.all_to_all(lifted_grid, 'slab', split_axis=1, concat_axis=0, tiled=True)]
    scatter-add x4 -> x0, other arithmetic: 601 us -> none  [the longest x1 517 us: shards(): cell_sum = jax.ops.segment_sum(terms, flat_cells, num_segments=slab_cells)]
    dot_general x25 -> x2, matrix products: 404 us -> 4.42 us  [the longest x1 3.28 us: shards(): jnp.einsum('wsarx,xdrbc->abcwsd', analysis, plane_sums, preferred_element...]
    all_to_all x10 -> x0, starting transfers between devices: 193 us -> none  [the longest x1 71.7 us: shards(): lax.all_to_all(cell_rows, 'slab', split_axis=0, concat_axis=0, tiled=True)]
    gather x5 -> x0, local copies, waits for them, and re-layouts: 174 us -> none  [the longest x1 149 us: shards(): cell_rows = hidden[flat_cells].reshape(slab_count, -1, C)]
    pallas_call x0 -> x7, Pallas kernels: none -> 159 us  [the longest x1 72.3 us: shards(): pl.pallas_call(share_kernel, out_shape=jax.ShapeDtypeStruct((lists, 1, CA...]
    convert_element_type x10 -> x3, local copies, waits for them, and re-layouts: 74.1 us -> 12.1 us  [the longest x1 8.78 us: shards(): coefficients = jnp.einsum('wsarx,xdrbc->abcwsd', analysis, plane_sums, pr...]
    reduce_scatter x0 -> x1, waiting for transfers between devices: none -> 50 us  [shards(): lax.psum_scatter(partial, 'slab', scatter_dimension=0, tiled=False)]
  transfers between devices with their start and end apart: 10 -> 2, of which waited for: 5 -> 1; matrix products, arithmetic and copies ran while one was open for 8% -> 1% of each run, Pallas kernels for 0% -> 26%
where the time goes in v1:
time: 319 us; the launch traced here: 318 us
  Pallas kernels  159 us (50%)
  local copies, waits for them, and re-layouts  61.3 us (19%)
  waiting for transfers between devices  50 us (16%)
  blocking collectives  25.5 us (8%)
  between operations  13.8 us (4%)
  matrix products  4.42 us (1%)
  other arithmetic  4.03 us (1%)
    pallas_call x1, Pallas kernels, shards(): pl.pallas_call(share_kernel, out_shape=jax.ShapeDtypeStruct((lists, 1, CA...  72.3 us
    reduce_scatter x1, waiting for transfers between devices, shards(): lax.psum_scatter(partial, 'slab', scatter_dimension=0, tiled=False)  50 us
    pallas_call x1, Pallas kernels, shards(): pl.pallas_call(mix_kernel, out_shape=jax.ShapeDtypeStruct((M, M, 8, C), F...  35.4 us
    all_gather x1, blocking collectives, shards(): all_meta = lax.all_gather(meta, 'slab')  25.5 us
    pallas_call x1, Pallas kernels, shards(): pl.pallas_call(functools.partial(forward_kernel, planes=planes), out_shap...  21.7 us
    mul x4, local copies, waits for them, and re-layouts, shards(): coefficients = coefficients[:, :, :, :, None] * same[:, None, :, None, None]  13.2 us
    pallas_call x1, Pallas kernels, shards(): pl.pallas_call(functools.partial(inverse_kernel, planes=planes), out_shap...  13 us
    reshape x2, local copies, waits for them, and re-layouts, shards(): plane_sums = plane_sums.reshape(G, C, 2, M, own_modes)  11.1 us
  transfers between devices with their start and end apart: 2, of which 1 were waited for; matrix products, arithmetic and copies ran while one was open for 1% of the time, Pallas kernels for 26%

profile of v1, /device:TPU:0, one launch (start us, length us, event | category | flops | bytes accessed | tf_op | source)
XLA Modules:
  0.0 317.9 jit_solution(14589221949294415898)
XLA Ops:
  6.5 0.0 all-gather.4.cloned.1.call-start
  6.5 0.8 fusion.48
  7.4 0.1 add_reduce_fusion
  7.5 0.1 select_reduce_fusion.2.own_slab_ref
  7.6 0.7 add_bitcast_fusion
  8.4 0.7 add_bitcast_fusion.1
  9.1 0.1 select_reduce_fusion
  9.2 0.1 concatenate.32.slab_ref
  9.3 0.0 copy-start.3
  9.3 0.9 copy-done.3
  10.3 0.0 copy-start.5
  10.3 0.8 copy-done.5
  11.0 0.0 copy-start.8
  11.0 0.7 copy-done.8
  11.7 3.7 %prep.1 = (bf16[64,1280]{1,0:T(8,128)(2,1)}, bf16[16,1280]{1,0:T(8,128)(2,1)S(1)}) custom-call(bf16[64,2048]{1,0:T(8,128)(2,1)S(1)} %bitcast.82, f32[3,2048]{1,0:T(4,128)S(1)} %copy-done.5, s32[8,256]{1,0:T(8,128)S(1)} %concatenate.29.point_ref, s32[8,256]{1,0:T(8,128)S(1)} %concatenate.30.cell_ref, s32[8,256]{1,0:T(8,128)S(1)} %concatenate.32.slab_ref, ...), custom_call_target="tpu_custom_call" | custom-call | tf_op jit(solution)/shard_map/prep/pallas_call | solution.py:263
  15.4 0.0 all-gather.4.cloned.1.call-update
  15.5 0.0 reduce-scatter.2.cloned.1.call-start
  15.5 25.5 %all-gather = bf16[256,1280]{1,0:T(8,128)(2,1)S(1)} all-gather(bf16[16,1280]{1,0:T(8,128)(2,1)S(1)} %get-tuple-element.9.meta_ref), channel_id=2, replica_groups=mesh['groups'=2,'slab'=16] {'slab'}, dimensions={0}, use_global_device_ids=true | all-gather | bytes 696320 | tf_op jit(solution)/shard_map/all_gather | solution.py:275
  41.0 0.1 slice.32
  41.1 0.1 slice.44
  41.2 0.1 convert_element_type.158
  41.4 0.1 mul.319
  41.5 0.1 mul.320
  41.6 0.1 reshape.535
  41.7 0.1 convert.64.weight_ref
  41.8 0.2 slice_add_fusion
  42.0 72.3 %share.1.share_ref = f32[80,1,256]{2,1,0:T(1,128)S(1)} custom-call(s32[80]{0:T(128)S(1)} %and_select_fusion.1.slab_ref, f32[80,1,256]{2,1,0:T(1,128)S(1)} %bitcast.80, f32[80,1,256]{2,1,0:T(1,128)S(1)} %convert.64.weight_ref), custom_call_target="tpu_custom_call" | custom-call | tf_op jit(solution)/shard_map/share/pallas_call | solution.py:287
  114.2 0.2 negate_bitcast_fusion
  114.4 0.2 fusion.33
  114.6 0.2 fusion.38
  114.8 0.1 cosine_convert_fusion
  114.9 0.2 fusion.37
  115.2 0.0 all-gather.4.cloned.1.call-done
  115.2 0.0 copy-start
  115.2 1.7 copy-done
  117.0 21.7 %forward.1 = (bf16[16,512,128]{2,1,0:T(8,128)(2,1)S(1)}, bf16[16,128,1280]{2,1,0:T(8,128)(2,1)}) custom-call(s32[80]{0:T(128)S(1)} %and_select_fusion.1.slab_ref, bf16[16,64,1280]{2,1,0:T(8,128)(2,1)S(1)} %bitcast.78, bf16[16,16,1280]{2,1,0:T(8,128)(2,1)S(1)} %bitcast.76, f32[80,1,256]{2,1,0:T(1,128)S(1)} %share.1.share_ref, ...), custom_call_target="tpu_custom_call" | custom-call | tf_op jit(solution)/shard_map/forward/pallas_call | solution.py:313
  138.7 3.0 copy.25
  141.6 6.3 %reshape.532 = bf16[128,64,2,32,2]{1,0,4,3,2:T(8,128)(2,1)} reshape(bf16[16,512,128]{1,0,2:T(8,128)(2,1)} %copy.25) | data formatting | bytes 4194304 | tf_op jit(solution)/shard_map/reshape | solution.py:341
  147.9 4.8 %copy.31 = bf16[128,64,2,32,2,1,1]{0,3,2,6,5,4,1:T(8,128)(2,1)S(1)} copy(bf16[128,64,2,32,2,1,1]{1,0,4,3,2,6,5:T(8,128)(2,1)} %bitcast.84) | data formatting | bytes 4194304 | tf_op jit(solution)/shard_map/reshape | solution.py:341
  152.7 3.3 %fusion = bf16[32,32,2,2,2,64]{0,1,4,3,2,5:T(8,128)(2,1)} fusion(bf16[128,64,2,32,2,1,1]{0,3,2,6,5,4,1:T(8,128)(2,1)S(1)} %copy.31, bf16[1,2,32,2,128]{4,2,3,1,0:T(8,128)(2,1)S(1)} %get-tuple-element.20, bf16[1,2,32,2,128]{4,2,3,1,0:T(8,128)(2,1)S(1)} %get-tuple-element.19), kind=kOutput, calls=%fused_computation.1 | convolution fusion | flops 269090816 | bytes 3211264 | tf_op jit(solution)/shard_map/wsarx,xdrbc->abcwsd/dot_general | solution.py:342
  156.0 8.8 %copy.27 = bf16[32,32,2,2,2,64]{5,4,3,2,1,0:T(2,128)(2,1)S(1)} copy(bf16[32,32,2,2,2,64]{0,1,4,3,2,5:T(8,128)(2,1)} %fusion) | data formatting | bytes 2097152 | tf_op jit(solution)/shard_map/convert_element_type | solution.py:344
  164.8 4.7 %mul.317 = bf16[32,32,2,2,2,2,64]{6,5,4,3,2,1,0:T(2,128)(2,1)} broadcast(bf16[32,32,2,2,2,64]{5,4,3,2,1,0:T(2,128)(2,1)S(1)} %copy.27), dimensions={0,1,2,3,5,6} | broadcast | bytes 3145728 | tf_op jit(solution)/shard_map/mul | solution.py:346
  169.4 8.4 %mul.318 = bf16[32,32,4,256]{3,2,1,0:T(4,128)(2,1)S(1)} reshape(bf16[32,32,2,2,2,2,64]{6,5,4,3,2,1,0:T(2,128)(2,1)} %mul.317) | data formatting | bytes 4194304 | tf_op jit(solution)/shard_map/mul | solution.py:346
  177.8 0.1 broadcast_multiply_fusion
  178.0 3.1 pad.8.coefficient_ref
  181.0 35.4 %mix.1 = f32[32,32,8,64]{3,2,1,0:T(8,128)S(1)} custom-call(bf16[32,32,8,256]{3,2,1,0:T(8,128)(2,1)} %pad.8.coefficient_ref, bf16[32,32,2,2,64,64]{5,4,3,2,1,0:T(8,128)(2,1)} %weight_ref.1), custom_call_target="tpu_custom_call" | custom-call | tf_op jit(solution)/shard_map/mix/pallas_call | solution.py:350
  216.5 0.3 slice.71
  216.8 1.1 fusion.1
  217.9 3.2 %copy.29 = bf16[128,64,2,32,2]{1,0,4,3,2:T(8,128)(2,1)} copy(bf16[128,64,2,32,2]{0,1,2,4,3:T(8,128)(2,1)S(1)} %fusion.1) | data formatting | bytes 4194304 | tf_op jit(solution)/shard_map/convert_element_type | solution.py:368
  221.2 6.4 %reshape.533 = bf16[16,512,128]{1,0,2:T(8,128)(2,1)} reshape(bf16[128,64,2,32,2]{1,0,4,3,2:T(8,128)(2,1)} %copy.29) | data formatting | bytes 4194304 | tf_op jit(solution)/shard_map/reshape | solution.py:369
  227.6 3.6 %copy.30.field_ref = bf16[16,512,128]{2,1,0:T(8,128)(2,1)S(1)} copy(bf16[16,512,128]{1,0,2:T(8,128)(2,1)} %reshape.533) | data formatting | bytes 4194304 | tf_op jit(solution)/shard_map/reshape | solution.py:369
  231.2 13.0 %inverse.1 = bf16[16,64,1280]{2,1,0:T(8,128)(2,1)S(1)} custom-call(s32[80]{0:T(128)S(1)} %and_select_fusion.1.slab_ref, bf16[16,16,1280]{2,1,0:T(8,128)(2,1)S(1)} %bitcast.77, bf16[16,128,1280]{2,1,0:T(8,128)(2,1)} %get-tuple-element.11.wave_ref, bf16[16,512,128]{2,1,0:T(8,128)(2,1)S(1)} %copy.30.field_ref), custom_call_target="tpu_custom_call" | custom-call | tf_op jit(solution)/shard_map/inverse/pallas_call | solution.py:371
  244.2 0.0 copy-start.2
  244.2 1.5 copy-done.2
  245.7 0.0 reduce-scatter.2.cloned.1.call-update
  245.7 0.0 copy-start.6
  245.7 0.0 copy-start.7
  245.8 1.6 copy-done.1
  247.4 9.7 %cells.1.cell_ref = f32[64,1280]{1,0:T(8,128)S(1)} custom-call(s32[80]{0:T(128)S(1)} %and_select_fusion.1.slab_ref, s32[5]{0:T(128)S(1)} %select_reduce_fusion.2.own_slab_ref, bf16[16,64,1280]{2,1,0:T(8,128)(2,1)S(1)} %bitcast.79, f32[80,1,256]{2,1,0:T(1,128)S(1)} %share.1.share_ref, f32[80,1,256]{2,1,0:T(1,128)S(1)} %bitcast.81, ...), custom_call_target="tpu_custom_call" | custom-call | tf_op jit(solution)/shard_map/cells/pallas_call | solution.py:385
  257.1 50.0 %reduce-scatter.2.cloned.1.call-done = bf16[1,64,1280]{2,1,0:T(8,128)(2,1)} async-done(((bf16[16,64,1280]{2,1,0:T(8,128)(2,1)}), bf16[1,64,1280]{2,1,0:T(8,128)(2,1)}) %reduce-scatter.2.cloned.1.call-update) | async-done | bytes 163856 | tf_op jit(solution)/shard_map/reduce_scatter | solution.py:383
  307.1 0.0 copy-done.6
  307.1 0.0 copy-done.7
  307.1 0.9 copy-done.4
  308.0 3.0 decode.1
  (29 shorter events, 0.3 us)
Async XLA Ops:
  6.5 108.7 %all-gather.4.cloned.1.call-start = ((), (), s32[]{:S(2)}) async-start(), calls=%async_computation.2 | async-start | bytes 2785280 | tf_op jit(solution)/shard_map/all_gather | solution.py:276
  9.3 1.0 copy-start.3
  10.3 0.8 copy-start.5
  11.0 0.7 copy-start.8
  15.5 291.7 %reduce-scatter.2.cloned.1.call-start = ((), (), s32[]{:S(2)}) async-start(), calls=%async_computation.1 | async-start | bytes 2785280 | tf_op jit(solution)/shard_map/reduce_scatter | solution.py:383
  115.2 1.7 copy-start
  244.2 1.5 copy-start.2
  245.7 1.7 copy-start.1
  245.7 61.4 %copy-start.6 = (bf16[64,64]{1,0:T(8,128)(2,1)S(1)}, bf16[64,64]{1,0:T(8,128)(2,1)}, u32[]{:S(2)}) copy-start(bf16[64,64]{1,0:T(8,128)(2,1)} %skip_ref.1) | copy-start | bytes 24580
  245.7 61.4 %copy-start.7 = (bf16[64,64]{1,0:T(8,128)(2,1)S(1)}, bf16[64,64]{1,0:T(8,128)(2,1)}, u32[]{:S(2)}) copy-start(bf16[64,64]{1,0:T(8,128)(2,1)} %proj_ref.1) | copy-start | bytes 24580
  307.1 0.9 copy-start.4
Sparse Core Ops, SparseCore 0:
  15.6 46.6 all-gather.3
  245.8 61.2 reduce-scatter.1

commit v2 on v1

--- a/solution.py
+++ b/solution.py
@@ -2,6 +2,7 @@
 
 import jax
 import jax.numpy as jnp
+import numpy as np
 from jax import lax
 from jax.experimental import pallas as pl
 from jax.experimental.pallas import tpu as pltpu
@@ -13,6 +14,7 @@
 RADIUS = 2
 LISTS = 5
 CAP = 256
+SIDE = 4
 VMEM_LIMIT = 48 * 1024 * 1024
 F32 = jnp.float32
 BF16 = jnp.bfloat16
@@ -77,51 +79,203 @@
         ).astype(BF16)
 
 
-def share_kernel(slab_ref, key_ref, weight_ref, share_ref, bucket, count):
+def places(slabs):
+    return (slabs // 4, 2) if slabs <= 16 else (slabs // 2, 1)
+
+
+def peers(depth, width):
+    me = lax.axis_index("slab")
+    core, y, z = me % 2, (me // 2) % width, me // (2 * width)
+
+    def at(z, y, core):
+        return (z * width + y) * 2 + core
+
+    return at, z, y, core
+
+
+def greet(others):
+    barrier = pltpu.get_barrier_semaphore()
+    for other in others:
+        pl.semaphore_signal(
+            barrier, inc=1, device_id={"slab": other}, device_id_type=pl.DeviceIdType.MESH
+        )
+    pl.semaphore_wait(barrier, len(others))
+
+
+def remote(source, target, send_sem, recv_sem, other):
+    return pltpu.make_async_remote_copy(
+        src_ref=source,
+        dst_ref=target,
+        send_sem=send_sem,
+        recv_sem=recv_sem,
+        device_id={"slab": other},
+        device_id_type=pl.DeviceIdType.MESH,
+    )
+
+
+def gather_kernel(source_ref, out_ref, send_sem, recv_sem, own_sem, depth, width):
+    at, z, y, core = peers(depth, width)
+    ahead = [at((z + d) % depth, y, core) for d in range(1, depth)]
+    beside = at(z, (y + 1) % width, core)
+    twin = at(z, y, 1 - core)
+    greet(ahead + ([beside] if width > 1 else []) + [twin])
+    me = at(z, y, core)
+    own = pltpu.make_async_copy(source_ref, out_ref.at[me], own_sem)
+    own.start()
+    sent = []
+
+    def send(source, block, other):
+        copy = remote(source, out_ref.at[block], send_sem.at[len(sent)], recv_sem.at[block], other)
+        copy.start()
+        sent.append(copy)
+
+    def arrived(block):
+        remote(source_ref, out_ref.at[block], send_sem.at[0], recv_sem.at[block], twin).wait_recv()
+
+    for other in ahead:
+        send(source_ref, me, other)
+    if width > 1:
+        send(source_ref, me, beside)
+    send(source_ref, me, twin)
+    for d in range(1, depth):
+        block = at((z + depth - d) % depth, y, core)
+        arrived(block)
+        if width > 1:
+            send(out_ref.at[block], block, beside)
+        send(out_ref.at[block], block, twin)
+    if width > 1:
+        for d in range(depth):
+            block = at((z + depth - d) % depth, 1 - y, core)
+            arrived(block)
+            send(out_ref.at[block], block, twin)
+    for d in range(depth):
+        for w in range(width):
+            arrived(at((z + depth - d) % depth, (y + w) % width, 1 - core))
+    own.wait()
+    for copy in sent:
+        copy.wait_send()
+
+
+def gather(block, slabs, collective_id, name):
+    depth, width = places(slabs)
+    return pl.pallas_call(
+        functools.partial(gather_kernel, depth=depth, width=width),
+        out_shape=jax.ShapeDtypeStruct((slabs,) + block.shape, block.dtype),
+        in_specs=[pl.BlockSpec(memory_space=pl.ANY)],
+        out_specs=pl.BlockSpec(memory_space=pl.ANY),
+        scratch_shapes=[
+            pltpu.SemaphoreType.DMA((slabs,)),
+            pltpu.SemaphoreType.DMA((slabs,)),
+            pltpu.SemaphoreType.DMA,
+        ],
+        compiler_params=pltpu.CompilerParams(collective_id=collective_id, has_side_effects=True),
+        name=name,
+    )(block)
+
+
+def scatter_kernel(
+    blocks_ref, out_ref, from_core, from_y, from_z, to_y, to_z,
+    core_send, core_recv, y_send, y_recv, z_send, z_recv, depth, width,
+):
+    at, z, y, core = peers(depth, width)
+    ahead = [at((z + d) % depth, y, core) for d in range(1, depth)]
+    beside = at(z, (y + 1) % width, core)
+    twin = at(z, y, 1 - core)
+    greet(ahead + ([beside] if width > 1 else []) + [twin])
+    order = list(range(1, depth)) + [0]
+    core_copies, y_copies, z_copies = {}, {}, {}
+    for d in order:
+        for w in reversed(range(width)):
+            slot = d * width + w
+            target = at((z + d) % depth, (y + w) % width, 1 - core)
+            core_copies[slot] = remote(
+                blocks_ref.at[target], from_core.at[slot], core_send.at[slot], core_recv.at[slot], twin
+            )
+            core_copies[slot].start()
+
+    def pair(d, w):
+        slot = d * width + w
+        core_copies[slot].wait_recv()
+        own = blocks_ref[at((z + d) % depth, (y + w) % width, core)].astype(F32)
+        return own + from_core[slot].astype(F32)
+
+    if width > 1:
+        for d in order:
+            to_y[d] = pair(d, 1).astype(BF16)
+            y_copies[d] = remote(to_y.at[d], from_y.at[d], y_send.at[d], y_recv.at[d], beside)
+            y_copies[d].start()
+    for d in order:
+        total = pair(d, 0)
+        if width > 1:
+            y_copies[d].wait_recv()
+            total += from_y[d].astype(F32)
+        if d > 0:
+            to_z[d] = total.astype(BF16)
+            z_copies[d] = remote(
+                to_z.at[d], from_z.at[d], z_send.at[d], z_recv.at[d], ahead[d - 1]
+            )
+            z_copies[d].start()
+        else:
+            out_ref[...] = total
+    for d in range(1, depth):
+        z_copies[d].wait_recv()
+        out_ref[...] += from_z[d].astype(F32)
+    for copies in (core_copies, y_copies, z_copies):
+        for copy in copies.values():
+            copy.wait_send()
+
+
+def scatter(blocks, slabs, collective_id, name):
+    depth, width = places(slabs)
+    shape = blocks.shape[1:]
+    return pl.pallas_call(
+        functools.partial(scatter_kernel, depth=depth, width=width),
+        out_shape=jax.ShapeDtypeStruct(shape, F32),
+        in_specs=[VMEM],
+        out_specs=VMEM,
+        scratch_shapes=[
+            pltpu.VMEM((depth * width,) + shape, BF16),
+            *[pltpu.VMEM((depth,) + shape, BF16)] * 4,
+            *[pltpu.SemaphoreType.DMA((depth * width,))] * 2,
+            *[pltpu.SemaphoreType.DMA((depth,))] * 4,
+        ],
+        compiler_params=pltpu.CompilerParams(
+            collective_id=collective_id, has_side_effects=True, vmem_limit_bytes=VMEM_LIMIT
+        ),
+        name=name,
+    )(blocks)
+
+
+def share_kernel(slab_ref, own_slab_ref, key_ref, weight_ref, own_key_ref, own_meta_ref, lifted_ref, term_ref, bucket, count):
     lists = key_ref.shape[0]
-    slabs = count.shape[0]
-
-    def clear(s, _):
-        count[s] = 0
-        return 0
-
-    lax.fori_loop(0, slabs, clear, 0)
-
-    def fill(i, _):
+    own = [own_slab_ref[k] for k in range(LISTS)]
+
+    def fill(i, counts):
         s = slab_ref[i]
-        n = count[s]
-        bucket[s * lists + n] = i
-        count[s] = n + 1
-        return 0
-
-    lax.fori_loop(0, lists, fill, 0)
-    share_ref[...] = jnp.zeros_like(share_ref)
-
-    def per_slab(s, _):
-        n = count[s]
-
-        def per_source(q, _):
-            j = bucket[s * lists + q]
-            both = jnp.concatenate([key_ref[j], weight_ref[j], jnp.zeros((6, CAP), F32)], axis=0)
+        for k in range(LISTS):
+            bucket[k * lists + counts[k]] = i
+        return tuple(n + (s == o).astype(jnp.int32) for n, o in zip(counts, own))
+
+    counts = lax.fori_loop(0, lists, fill, (jnp.int32(0),) * LISTS)
+    for k in range(LISTS):
+        count[k] = counts[k]
+        place = pl.ds(k * CAP, CAP)
+        own_key = own_key_ref[k : k + 1, :]
+
+        def add(p, total):
+            i = bucket[k * lists + p]
+            both = jnp.concatenate([key_ref[i], weight_ref[i], jnp.zeros((6, CAP), F32)], axis=0)
             turned = both.T
-            key = turned[:, 0:1]
-            weight = turned[:, 1:2]
-
-            def per_target(p, _):
-                i = bucket[s * lists + p]
-                terms = jnp.where(key == key_ref[i], weight, 0.0)
-                share_ref[i] += jnp.sum(terms, axis=0, keepdims=True)
-                return 0
-
-            return lax.fori_loop(0, n, per_target, 0)
-
-        return lax.fori_loop(0, n, per_source, 0)
-
-    lax.fori_loop(0, slabs, per_slab, 0)
-    share_ref[...] = weight_ref[...] / (1.0 + share_ref[...])
-
-
-def forward_kernel(slab_ref, lifted_ref, meta_ref, share_ref, tab_y_ref, tab_z_ref, planes_ref, wave_ref, total, planes):
+            terms = jnp.where(turned[:, 0:1] == own_key, turned[:, 1:2], 0.0)
+            return total + jnp.sum(terms, axis=0, keepdims=True)
+
+        total = lax.fori_loop(0, counts[k], add, jnp.zeros((1, CAP), F32))
+        weight = own_meta_ref[:, place].astype(F32)[3:4]
+        scaled = lifted_ref[:, place].astype(F32) * (weight / (1.0 + total))
+        term_ref[:, place] = scaled.astype(BF16)
+
+
+def forward_kernel(slab_ref, lifted_ref, meta_ref, tab_y_ref, tab_z_ref, tab_x_ref, modes_ref, wave_ref, total, lines, planes):
     region = pl.program_id(0)
     rows = wave_ref.shape[1]
 
@@ -141,59 +295,103 @@
         wave = along_y[:rows] * along_z[:rows] + along_y[rows:] * along_z[rows:]
         wave = wave.astype(BF16)
         wave_ref[0, :, place] = wave
-        scaled = (lifted_ref[0, :, place].astype(F32) * share_ref[k]).astype(BF16)
+        scaled = lifted_ref[0, :, place]
         local = meta[0:1] - (slab * planes).astype(F32)
         parts = [
             scaled * jnp.where(local == float(p), 1.0, 0.0).astype(BF16) for p in range(planes)
         ]
-        total[slab] += nt_dot(jnp.concatenate(parts, axis=0), wave)
+        height = planes * C
+        at = pl.ds(pl.multiple_of(slab * height, height), height)
+        total[at, :] += nt_dot(jnp.concatenate(parts, axis=0), wave)
 
     @pl.when(region == pl.num_programs(0) - 1)
     def _():
-        planes_ref[...] = total[...].astype(BF16)
-
-
-def mix_kernel(coefficient_ref, weight_ref, out_ref):
-    columns, depth = weight_ref.shape[1], coefficient_ref.shape[-1]
-    for b in range(columns):
-        weights = weight_ref[0, b].reshape(depth, C)
-        out_ref[0, b] = dot(coefficient_ref[0, b], weights)
-
-
-def inverse_kernel(slab_ref, meta_ref, wave_ref, field_ref, out_ref, planes):
+        half = rows // 2
+        sign = jnp.where(lax.broadcasted_iota(jnp.int32, (M, rows), 1) < half, 1.0, -1.0)
+
+        def along_x(d, _):
+            line = total[pl.ds(d, G, stride=C), :].astype(BF16)
+            both = dot(tab_x_ref[...], line)
+            turned = jnp.concatenate([both[M:, half:], both[M:, :half]], axis=1)
+            lines[pl.ds(pl.multiple_of(d * M, M), M), :] = both[:M] + sign * turned
+            return 0
+
+        lax.fori_loop(0, C, along_x, 0, unroll=16)
+        for a in range(M):
+            modes_ref[a] = lines[pl.ds(a, C, stride=M), :].astype(BF16)
+
+
+def mix_kernel(modes_ref, weight_ref, spread_ref, collect_ref, out_ref, products):
+    columns, own_modes = weight_ref.shape[1], weight_ref.shape[2]
+    depth, height = own_modes * 2 * C, own_modes * 2 * SIDE
+    modes = modes_ref[0]
+    sides = [nt_dot(spread_ref[i], modes) for i in range(spread_ref.shape[0])]
+    left = jnp.concatenate(sides, axis=1)
+    for g in range(columns // SIDE):
+        weights = [weight_ref[0, SIDE * g + i].reshape(depth, C) for i in range(SIDE)]
+        rows = slice(height * g, height * (g + 1))
+        products[rows, :] = dot(left[rows].astype(BF16), jnp.concatenate(weights, axis=1))
+    turned = lax.dot_general(
+        products[...].astype(BF16),
+        collect_ref[...],
+        (((0,), (0,)), ((), ())),
+        preferred_element_type=F32,
+    )
+    lane = lax.broadcasted_iota(jnp.int32, (C, turned.shape[1]), 1)
+    side = lane // own_modes % SIDE
+    total = turned[:C]
+    for i in range(1, SIDE):
+        total = jnp.where(side == i, turned[i * C : (i + 1) * C], total)
+    out_ref[0] = total
+
+
+def inverse_kernel(slab_ref, meta_ref, wave_ref, mixed_ref, tab_x_ref, out_ref, lines, field, planes):
     region = pl.program_id(0)
+    rows = wave_ref.shape[1]
+    height = planes * C
+
+    @pl.when(region == 0)
+    def _():
+        half = rows // 2
+        sign = jnp.where(lax.broadcasted_iota(jnp.int32, (M, rows), 1) < half, -1.0, 1.0)
+
+        def along_x(e, _):
+            line = mixed_ref[pl.ds(e, M, stride=C), :]
+            turned = sign * jnp.concatenate([line[:, half:], line[:, :half]], axis=1)
+            both = jnp.concatenate([line, turned], axis=0).astype(BF16)
+            lines[pl.ds(e, G, stride=C), :] = dot(tab_x_ref[...], both)
+            return 0
+
+        lax.fori_loop(0, C, along_x, 0, unroll=16)
+        field[...] = lines[...].astype(BF16)
+
     for k in range(LISTS):
         place = pl.ds(k * CAP, CAP)
         slab = slab_ref[region * LISTS + k]
         local = meta_ref[0, :, place].astype(F32)[0:1] - (slab * planes).astype(F32)
-        values = dot(field_ref[slab], wave_ref[0, :, place])
+        at = pl.ds(pl.multiple_of(slab * height, height), height)
+        values = dot(field[at, :], wave_ref[0, :, place])
         total = jnp.zeros((C, CAP), F32)
         for p in range(planes):
             total += jnp.where(local == float(p), values[p * C : (p + 1) * C], 0.0)
         out_ref[0, :, place] = total.astype(BF16)
 
 
-def cell_kernel(slab_ref, own_slab_ref, lifted_ref, share_ref, key_ref, own_key_ref, out_ref):
-    regions = lifted_ref.shape[0]
+def cell_kernel(bucket, count, lifted_ref, key_ref, own_key_ref, out_ref):
+    lists = key_ref.shape[0]
     for k in range(LISTS):
-        place = pl.ds(k * CAP, CAP)
-        out_ref[:, place] = jnp.zeros((C, CAP), F32)
         own = own_key_ref[k : k + 1, :]
         turned = jnp.broadcast_to(own, (8, CAP)).T[:, 0:1]
-        slab = own_slab_ref[k]
-
-        def per_region(r, _):
-            for m in range(LISTS):
-
-                @pl.when(slab_ref[r * LISTS + m] == slab)
-                def _():
-                    same = jnp.where(turned == key_ref[r * LISTS + m], 1.0, 0.0).astype(BF16)
-                    terms = lifted_ref[r, :, pl.ds(m * CAP, CAP)].astype(F32) * share_ref[r * LISTS + m]
-                    out_ref[:, place] += nt_dot(terms.astype(BF16), same)
-
-            return 0
-
-        lax.fori_loop(0, regions, per_region, 0)
+
+        def add(p, total):
+            i = bucket[k * lists + p]
+            same = jnp.where(turned == key_ref[i], 1.0, 0.0).astype(BF16)
+            slots = pl.ds(pl.multiple_of((i % LISTS) * CAP, CAP), CAP)
+            return total + nt_dot(lifted_ref[i // LISTS, :, slots], same)
+
+        out_ref[:, pl.ds(k * CAP, CAP)] = lax.fori_loop(
+            0, count[k], add, jnp.zeros((C, CAP), F32)
+        )
 
 
 def decode_kernel(spectral_ref, cell_ref, meta_ref, point_ref, skip_ref, proj_ref, out_ref):
@@ -220,6 +418,22 @@
     ).astype(BF16)
 
 
+def selections(own_modes):
+    spread = np.zeros((own_modes, 2, M, 2 * own_modes, 2, M, own_modes), np.float32)
+    collect = np.zeros((M, 2 * own_modes, 2, M, own_modes), np.float32)
+    for b in range(M):
+        for c in range(own_modes):
+            for w in range(2):
+                collect[b, 2 * c + w, w, b, c] = 1.0
+                for s in range(2):
+                    spread[c, s, b, 2 * c + w, s ^ w, b, c] = -1.0 if s > w else 1.0
+    rows = 2 * M * own_modes
+    return (
+        jnp.asarray(spread.reshape(2 * own_modes, rows, rows), BF16),
+        jnp.asarray(collect.reshape(rows, rows), BF16),
+    )
+
+
 def compact(lists, live):
     rank = jnp.cumsum(live.astype(jnp.int32)) - 1
     hot = live[None, :] & (rank[None, :] == jnp.arange(LISTS)[:, None])
@@ -272,8 +486,7 @@
         name="prep",
     )(point_feat.T, point_pos, point_ids, cells, pad8(slab_rows), lift_weight)
 
-    all_meta = lax.all_gather(meta, "slab")
-    all_lifted = lax.all_gather(lifted, "slab")
+    all_meta = gather(meta, slabs, 0, "gather_meta")
 
     def keys(values):
         values = values.astype(F32)
@@ -284,18 +497,19 @@
     slab_ids = (all_meta[:, 0, ::CAP].astype(jnp.int32) // planes).reshape(lists)
     own_key = pad8(keys(meta).reshape(LISTS, CAP))
 
-    share = pl.pallas_call(
+    terms, bucket, count = pl.pallas_call(
         share_kernel,
-        out_shape=jax.ShapeDtypeStruct((lists, 1, CAP), F32),
-        in_specs=[SMEM, VMEM, VMEM],
-        out_specs=VMEM,
-        scratch_shapes=[
-            pltpu.SMEM((slabs * lists,), jnp.int32),
-            pltpu.SMEM((slabs,), jnp.int32),
-        ],
+        out_shape=(
+            jax.ShapeDtypeStruct((C, slots), BF16),
+            jax.ShapeDtypeStruct(((LISTS + 1) * lists,), jnp.int32),
+            jax.ShapeDtypeStruct((LISTS,), jnp.int32),
+        ),
+        in_specs=[SMEM, SMEM, VMEM, VMEM, VMEM, VMEM, VMEM],
+        out_specs=(VMEM, SMEM, SMEM),
         compiler_params=params(),
         name="share",
-    )(slab_ids, key, weight)
+    )(slab_ids, own_slab, key, weight, own_key, meta, lifted)
+    all_terms = gather(terms, slabs, 1, "gather_terms")
 
     cos_y, sin_y = waves(frequencies(M), G)
     cos_z, sin_z = waves(frequencies(own_modes, me * own_modes), G)
@@ -310,10 +524,11 @@
     def whole(shape):
         return pl.BlockSpec(shape, lambda r, ids: (0,) * len(shape))
 
-    plane_sums, wave = pl.pallas_call(
+    tab_x = jnp.concatenate([cos_y, sin_y], 0)
+    modes, wave = pl.pallas_call(
         functools.partial(forward_kernel, planes=planes),
         out_shape=(
-            jax.ShapeDtypeStruct((slabs, planes * C, rows), BF16),
+            jax.ShapeDtypeStruct((M, C, rows), BF16),
             jax.ShapeDtypeStruct((slabs, rows, slots), BF16),
         ),
         grid_spec=pltpu.PrefetchScalarGridSpec(
@@ -322,51 +537,33 @@
             in_specs=[
                 region_block(C),
                 region_block(16),
-                pl.BlockSpec((LISTS, 1, CAP), lambda r, ids: (r, 0, 0)),
                 whole((2 * rows, G)),
                 whole((2 * rows, G)),
+                whole((2 * M, G)),
             ],
-            out_specs=(whole((slabs, planes * C, rows)), region_block(rows)),
-            scratch_shapes=[pltpu.VMEM((slabs, planes * C, rows), F32)],
+            out_specs=(whole((M, C, rows)), region_block(rows)),
+            scratch_shapes=[pltpu.VMEM((G * C, rows), F32), pltpu.VMEM((C * M, rows), F32)],
         ),
         compiler_params=params(),
         name="forward",
-    )(slab_ids, all_lifted, all_meta, share, tab_y, tab_z)
-
-    real_row = jnp.stack([cos_y, sin_y], 1)
-    imag_row = jnp.stack([-sin_y, cos_y], 1)
-    analysis = jnp.stack(
-        [jnp.stack([real_row, -imag_row]), jnp.stack([imag_row, real_row])]
-    ).astype(BF16)
-    plane_sums = plane_sums.reshape(G, C, 2, M, own_modes)
-    coefficients = jnp.einsum(
-        "wsarx,xdrbc->abcwsd", analysis, plane_sums, preferred_element_type=F32
-    ).astype(BF16)
-    same = jnp.eye(own_modes, dtype=BF16)
-    coefficients = coefficients[:, :, :, :, None] * same[:, None, :, None, None]
-    coefficients = coefficients.reshape(M, M, 2 * own_modes, own_modes * 2 * C)
-    coefficients = jnp.pad(coefficients, ((0, 0), (0, 0), (0, 8 - 2 * own_modes), (0, 0)))
-
-    filtered = pl.pallas_call(
+    )(slab_ids, all_terms, all_meta, tab_y, tab_z, tab_x.astype(BF16))
+
+    spread, collect = selections(own_modes)
+    mixed = pl.pallas_call(
         mix_kernel,
-        out_shape=jax.ShapeDtypeStruct((M, M, 8, C), F32),
+        out_shape=jax.ShapeDtypeStruct((M, C, rows), F32),
         grid=(M,),
         in_specs=[
-            pl.BlockSpec((1, M, 8, own_modes * 2 * C), lambda a: (a, 0, 0, 0)),
+            pl.BlockSpec((1, C, rows), lambda a: (a, 0, 0)),
             pl.BlockSpec((1, M, own_modes, 2, C, C), lambda a: (a, 0, 0, 0, 0, 0)),
+            pl.BlockSpec(spread.shape, lambda a: (0, 0, 0)),
+            pl.BlockSpec(collect.shape, lambda a: (0, 0)),
         ],
-        out_specs=pl.BlockSpec((1, M, 8, C), lambda a: (a, 0, 0, 0)),
+        out_specs=pl.BlockSpec((1, C, rows), lambda a: (a, 0, 0)),
+        scratch_shapes=[pltpu.VMEM((2 * own_modes * M, SIDE * C), F32)],
         compiler_params=params(),
         name="mix",
-    )(coefficients, spectral_weight)
-
-    filtered = filtered[:, :, : 2 * own_modes].reshape(M, M, own_modes, 2, C).astype(BF16)
-    synthesis = jnp.stack([jnp.stack([cos_y, -sin_y]), jnp.stack([sin_y, cos_y])])
-    synthesis = (synthesis / float(G * G * G)).astype(BF16)
-    field = jnp.einsum(
-        "rwax,abcwe->xerbc", synthesis, filtered, preferred_element_type=F32
-    ).astype(BF16)
-    field = field.reshape(slabs, planes * C, rows)
+    )(modes, spectral_weight, spread, collect)
 
     partial = pl.pallas_call(
         functools.partial(inverse_kernel, planes=planes),
@@ -374,22 +571,28 @@
         grid_spec=pltpu.PrefetchScalarGridSpec(
             num_scalar_prefetch=1,
             grid=(slabs,),
-            in_specs=[region_block(16), region_block(rows), whole((slabs, planes * C, rows))],
+            in_specs=[
+                region_block(16),
+                region_block(rows),
+                whole((M * C, rows)),
+                whole((G, 2 * M)),
+            ],
             out_specs=region_block(C),
+            scratch_shapes=[pltpu.VMEM((G * C, rows), F32), pltpu.VMEM((G * C, rows), BF16)],
         ),
         compiler_params=params(),
         name="inverse",
-    )(slab_ids, all_meta, wave, field)
-    spectral = lax.psum_scatter(partial, "slab", scatter_dimension=0, tiled=False)
+    )(slab_ids, all_meta, wave, mixed.reshape(M * C, rows), (tab_x.T / float(G * G * G)).astype(BF16))
+    spectral = scatter(partial, slabs, 2, "scatter")
 
     cell_lifted = pl.pallas_call(
         cell_kernel,
         out_shape=jax.ShapeDtypeStruct((C, slots), F32),
-        in_specs=[SMEM, SMEM, VMEM, VMEM, VMEM, VMEM],
+        in_specs=[SMEM, SMEM, VMEM, VMEM, VMEM],
         out_specs=VMEM,
         compiler_params=params(),
         name="cells",
-    )(slab_ids, own_slab, all_lifted, share, key, own_key)
+    )(bucket, count, all_terms, key, own_key)
 
     out = pl.pallas_call(
         decode_kernel,

time: 319 us -> 191 us (0.60)
  local copies, waits for them, and re-layouts: 61.3 us -> 8.24 us
  waiting for transfers between devices: 50 us -> 0 us
  blocking collectives: 25.5 us -> 0 us
  Pallas kernels: 159 us -> 176 us
  between operations: 13.8 us -> 0.37 us
  matrix products: 4.42 us -> 0 us
    reduce_scatter x1 -> x0, waiting for transfers between devices: 50 us -> none  [shards(): lax.psum_scatter(partial, 'slab', scatter_dimension=0, tiled=False)]
    all_gather x1 -> x0, blocking collectives: 25.5 us -> none  [shards(): all_meta = lax.all_gather(meta, 'slab')]
    reshape x4 -> x0, local copies, waits for them, and re-layouts: 21 us -> none  [the longest x2 11.1 us: shards(): plane_sums = plane_sums.reshape(G, C, 2, M, own_modes)]
    mul x4 -> x0, local copies, waits for them, and re-layouts: 13.2 us -> none  [shards(): coefficients = coefficients[:, :, :, :, None] * same[:, None, :, None, None]]
    convert_element_type x2, local copies, waits for them, and re-layouts: 12 us -> 0.18 us  [the longest x1 0.1 us: waves(): angle = 2.0 * jnp.pi / length * phase.astype(F32)]
    pallas_call x2 -> x5, Pallas kernels: 108 us -> 119 us  [the longest x2 40.6 us: gather(): pl.pallas_call(functools.partial(gather_kernel, depth=depth, width=width)...]
    pallas_call x1, Pallas kernels: 13 us -> 17.5 us  [shards(): pl.pallas_call(functools.partial(inverse_kernel, planes=planes), out_shap...]
    dot_general x2 -> x0, matrix products: 4.42 us -> none  [the longest x1 3.28 us: shards(): jnp.einsum('wsarx,xdrbc->abcwsd', analysis, plane_sums, preferred_element...]
  transfers between devices with their start and end apart: 2 -> 0, of which waited for: 1 -> 0; matrix products, arithmetic and copies ran while one was open for 1% -> 0% of each run, Pallas kernels for 26% -> 0%
where the time goes in v2:
time: 191 us; the launch traced here: 189 us
  Pallas kernels  176 us (92%)
  local copies, waits for them, and re-layouts  8.24 us (4%)
  other arithmetic  4.83 us (3%)
    pallas_call x2, Pallas kernels, gather(): pl.pallas_call(functools.partial(gather_kernel, depth=depth, width=width)...  40.6 us
    pallas_call x1, Pallas kernels, shards(): pl.pallas_call(mix_kernel, out_shape=jax.ShapeDtypeStruct((M, C, rows), F...  38.9 us
    pallas_call x1, Pallas kernels, scatter(): pl.pallas_call(functools.partial(scatter_kernel, depth=depth, width=width...  28.7 us
    pallas_call x1, Pallas kernels, shards(): pl.pallas_call(functools.partial(forward_kernel, planes=planes), out_shap...  25.2 us
    pallas_call x1, Pallas kernels, shards(): pl.pallas_call(functools.partial(inverse_kernel, planes=planes), out_shap...  17.5 us
    pallas_call x1, Pallas kernels, shards(): pl.pallas_call(share_kernel, out_shape=(jax.ShapeDtypeStruct((C, slots),...  10.5 us
    pallas_call x1, Pallas kernels, shards(): pl.pallas_call(cell_kernel, out_shape=jax.ShapeDtypeStruct((C, slots), F3...  7.81 us
    unnamed x26, local copies, waits for them, and re-layouts  5.39 us

profile of v2, /device:TPU:0, one launch (start us, length us, event | category | flops | bytes accessed | tf_op | source)
XLA Modules:
  0.0 189.3 jit_solution(7280079839041675210)
XLA Ops:
  0.0 0.1 cosine_convert_fusion
  0.1 0.8 fusion.15
  1.0 0.1 add_reduce_fusion
  1.1 0.1 select_reduce_fusion.2.own_slab_ref
  1.2 0.1 concatenate.28.slab_ref
  1.3 0.1 fusion.4
  1.4 0.7 add_bitcast_fusion.1
  2.1 0.7 add_bitcast_fusion
  2.8 0.1 select_reduce_fusion
  3.0 0.1 copy.27
  3.1 0.3 multiply_cosine_fusion
  3.4 0.1 copy.28
  3.5 0.1 copy.30
  3.6 0.1 copy.29
  3.7 0.1 fusion.2
  3.8 0.1 fusion.1.tab_x_ref
  3.9 0.1 copy.31.tab_x_ref
  4.0 0.0 copy-start.5
  4.0 0.9 copy-done.5
  5.0 0.0 copy-start.9
  5.0 0.8 copy-done.9
  5.7 0.0 copy-start.12
  5.7 0.7 copy-done.12
  6.5 3.7 %prep.1 = (bf16[64,1280]{1,0:T(8,128)(2,1)S(1)}, bf16[16,1280]{1,0:T(8,128)(2,1)S(1)}) custom-call(bf16[64,2048]{1,0:T(8,128)(2,1)S(1)} %bitcast.22, f32[3,2048]{1,0:T(4,128)S(1)} %copy-done.9, s32[8,256]{1,0:T(8,128)S(1)} %concatenate.25.point_ref, s32[8,256]{1,0:T(8,128)S(1)} %concatenate.26.cell_ref, s32[8,256]{1,0:T(8,128)S(1)} %concatenate.28.slab_ref, ...), custom_call_target="tpu_custom_call" | custom-call | tf_op jit(solution)/shard_map/prep/pallas_call | solution.py:477
  10.2 0.0 copy-start.3
  10.3 0.5 copy-done.3
  10.8 15.2 %gather_meta.1.meta_ref = bf16[16,16,1280]{2,1,0:T(8,128)(2,1)} custom-call(bf16[16,1280]{1,0:T(8,128)(2,1)} %copy-done.3), custom_call_target="tpu_custom_call" | custom-call | tf_op jit(solution)/shard_map/gather_meta/pallas_call | solution.py:161
  26.0 0.0 copy-start.4
  26.0 1.1 slice.28
  27.1 0.1 reshape.230
  27.2 1.1 slice.32
  28.3 0.1 convert.36.weight_ref
  28.4 1.2 convert_element_type.79
  29.6 0.2 slice_add_fusion
  29.8 0.0 copy-done.4
  29.8 10.5 %share.1 = (bf16[64,1280]{1,0:T(8,128)(2,1)S(1)}, s32[480]{0:T(512)S(1)}, s32[5]{0:T(128)S(1)}) custom-call(s32[80]{0:T(128)S(1)} %and_select_fusion.1.slab_ref, s32[5]{0:T(128)S(1)} %select_reduce_fusion.2.own_slab_ref, f32[80,1,256]{2,1,0:T(1,128)S(1)} %bitcast.20, f32[80,1,256]{2,1,0:T(1,128)S(1)} %convert.36.weight_ref, ...), custom_call_target="tpu_custom_call" | custom-call | tf_op jit(solution)/shard_map/share/pallas_call | solution.py:500
  40.3 0.0 copy-start.6
  40.3 0.7 copy-done.6
  41.0 0.0 copy-start.2
  41.0 25.4 %gather_terms.1.lifted_ref = bf16[16,64,1280]{2,1,0:T(8,128)(2,1)} custom-call(bf16[64,1280]{1,0:T(8,128)(2,1)} %copy-done.6), custom_call_target="tpu_custom_call" | custom-call | tf_op jit(solution)/shard_map/gather_terms/pallas_call | solution.py:161
  66.4 0.0 copy-start
  66.4 1.7 copy-done
  68.1 0.0 copy-start.1
  68.1 0.0 copy-start.7
  68.1 0.0 copy-start.8
  68.1 7.8 %cells.1.cell_ref = f32[64,1280]{1,0:T(8,128)S(1)} custom-call(s32[480]{0:T(512)S(1)} %get-tuple-element.17.bucket, s32[5]{0:T(128)S(1)} %get-tuple-element.18.count, bf16[16,64,1280]{2,1,0:T(8,128)(2,1)S(1)} %copy-done, f32[80,1,256]{2,1,0:T(1,128)S(1)} %bitcast.21, f32[8,256]{1,0:T(8,128)S(1)} %concatenate.29.own_key_ref), custom_call_target="tpu_custom_call" | custom-call | tf_op jit(solution)/shard_map/cells/pallas_call | solution.py:588
  76.0 0.0 copy-done.2
  76.0 0.0 copy-done.1
  76.0 25.2 %forward.1 = (bf16[32,64,128]{2,1,0:T(8,128)(2,1)S(1)}, bf16[16,128,1280]{2,1,0:T(8,128)(2,1)}) custom-call(s32[80]{0:T(128)S(1)} %and_select_fusion.1.slab_ref, bf16[16,64,1280]{2,1,0:T(8,128)(2,1)S(1)} %copy-done.1, bf16[16,16,1280]{2,1,0:T(8,128)(2,1)S(1)} %copy-done.2, bf16[256,128]{1,0:T(8,128)(2,1)S(1)} %get-tuple-element.32.tab_y_ref, ...), custom_call_target="tpu_custom_call" | custom-call | tf_op jit(solution)/shard_map/forward/pallas_call | solution.py:528
  101.1 0.0 copy-done.7
  101.1 0.0 copy-done.8
  101.1 38.9 %mix.1 = f32[32,64,128]{2,1,0:T(8,128)S(1)} custom-call(bf16[32,64,128]{2,1,0:T(8,128)(2,1)S(1)} %get-tuple-element.16.modes_ref, bf16[32,32,2,2,64,64]{5,4,3,2,1,0:T(8,128)(2,1)} %weight_ref.1, bf16[4,128,128]{2,1,0:T(8,128)(2,1)S(1)} %copy-done.7, bf16[128,128]{1,0:T(8,128)(2,1)S(1)} %copy-done.8), custom_call_target="tpu_custom_call" | custom-call | tf_op jit(solution)/shard_map/mix/pallas_call | solution.py:552
  140.1 17.5 %inverse.1.blocks_ref = bf16[16,64,1280]{2,1,0:T(8,128)(2,1)S(1)} custom-call(s32[80]{0:T(128)S(1)} %and_select_fusion.1.slab_ref, bf16[16,16,1280]{2,1,0:T(8,128)(2,1)S(1)} %copy-done.2, bf16[16,128,1280]{2,1,0:T(8,128)(2,1)} %get-tuple-element.15.wave_ref, f32[2048,128]{1,0:T(8,128)S(1)} %bitcast.19, bf16[128,64]{1,0:T(8,128)(2,1)S(1)} %fusion.1.tab_x_ref), custom_call_target="tpu_custom_call" | custom-call | tf_op jit(solution)/shard_map/inverse/pallas_call | solution.py:568
  157.6 0.0 copy-start.10
  157.6 0.0 copy-start.11
  157.6 28.7 %scatter.1.spectral_ref = f32[64,1280]{1,0:T(8,128)S(1)} custom-call(bf16[16,64,1280]{2,1,0:T(8,128)(2,1)S(1)} %inverse.1.blocks_ref), custom_call_target="tpu_custom_call" | custom-call | tf_op jit(solution)/shard_map/scatter/pallas_call | solution.py:231
  186.3 0.0 copy-done.10
  186.3 0.0 copy-done.11
  186.3 3.0 %decode.1 = bf16[64,2048]{1,0:T(8,128)(2,1)} custom-call(f32[64,1280]{1,0:T(8,128)S(1)} %scatter.1.spectral_ref, f32[64,1280]{1,0:T(8,128)S(1)} %cells.1.cell_ref, bf16[16,1280]{1,0:T(8,128)(2,1)S(1)} %copy-done.4, s32[8,256]{1,0:T(8,128)S(1)} %concatenate.25.point_ref, bf16[64,64]{1,0:T(8,128)(2,1)S(1)} %copy-done.10, bf16[64,64]{1,0:T(8,128)(2,1)S(1)} %copy-done.11), custom_call_target="tpu_custom_call" | custom-call | tf_op jit(solution)/shard_map/decode/pallas_call | solution.py:597
  (21 shorter events, 0.3 us)
Async XLA Ops:
  4.0 1.0 copy-start.5
  5.0 0.8 copy-start.9
  5.7 0.7 copy-start.12
  10.2 0.6 copy-start.3
  26.0 3.8 %copy-start.4 = (bf16[16,1280]{1,0:T(8,128)(2,1)S(1)}, bf16[16,1280]{1,0:T(8,128)(2,1)}, u32[]{:S(2)}) copy-start(bf16[16,1280]{1,0:T(8,128)(2,1)} %copy-done.3) | copy-start | bytes 122884
  40.3 0.7 copy-start.6
  41.0 34.9 %copy-start.2 = (bf16[16,16,1280]{2,1,0:T(8,128)(2,1)S(1)}, bf16[16,16,1280]{2,1,0:T(8,128)(2,1)}, u32[]{:S(2)}) copy-start(bf16[16,16,1280]{2,1,0:T(8,128)(2,1)} %gather_meta.1.meta_ref) | copy-start | bytes 1966084
  66.4 1.7 copy-start
  68.1 7.8 %copy-start.1 = (bf16[16,64,1280]{2,1,0:T(8,128)(2,1)S(1)}, bf16[16,64,1280]{2,1,0:T(8,128)(2,1)}, u32[]{:S(2)}) copy-start(bf16[16,64,1280]{2,1,0:T(8,128)(2,1)} %gather_terms.1.lifted_ref) | copy-start | bytes 7864324
  68.1 33.0 %copy-start.7 = (bf16[4,128,128]{2,1,0:T(8,128)(2,1)S(1)}, bf16[4,128,128]{2,1,0:T(8,128)(2,1)}, u32[]{:S(2)}) copy-start(bf16[4,128,128]{2,1,0:T(8,128)(2,1)} %constant.80.clone.spread_ref) | copy-start | bytes 393220
  68.1 33.0 %copy-start.8 = (bf16[128,128]{1,0:T(8,128)(2,1)S(1)}, bf16[128,128]{1,0:T(8,128)(2,1)}, u32[]{:S(2)}) copy-start(bf16[128,128]{1,0:T(8,128)(2,1)} %constant.81.clone.collect_ref) | copy-start | bytes 98308
  157.6 28.7 %copy-start.10 = (bf16[64,64]{1,0:T(8,128)(2,1)S(1)}, bf16[64,64]{1,0:T(8,128)(2,1)}, u32[]{:S(2)}) copy-start(bf16[64,64]{1,0:T(8,128)(2,1)} %skip_ref.1) | copy-start | bytes 24580
  157.6 28.7 %copy-start.11 = (bf16[64,64]{1,0:T(8,128)(2,1)S(1)}, bf16[64,64]{1,0:T(8,128)(2,1)}, u32[]{:S(2)}) copy-start(bf16[64,64]{1,0:T(8,128)(2,1)} %proj_ref.1) | copy-start | bytes 24580

commit v3 on v2

--- a/solution.py
+++ b/solution.py
@@ -14,14 +14,17 @@
 RADIUS = 2
 LISTS = 5
 CAP = 256
+HELD = 20
+STEP = 4
 SIDE = 4
-VMEM_LIMIT = 48 * 1024 * 1024
+VMEM_LIMIT = 32 * 1024 * 1024
+VMEM_MOST = 58 * 1024 * 1024
 F32 = jnp.float32
 BF16 = jnp.bfloat16
 
 
-def params():
-    return pltpu.CompilerParams(vmem_limit_bytes=VMEM_LIMIT)
+def params(limit=VMEM_LIMIT):
+    return pltpu.CompilerParams(vmem_limit_bytes=limit)
 
 
 def frequencies(count, first=0):
@@ -259,28 +262,73 @@
     counts = lax.fori_loop(0, lists, fill, (jnp.int32(0),) * LISTS)
     for k in range(LISTS):
         count[k] = counts[k]
+    own_keys = [own_key_ref[k : k + 1, :] for k in range(LISTS)]
+
+    def add(p, totals):
+        added = []
+        for k in range(LISTS):
+            valid = p < counts[k]
+            i = jnp.where(valid, bucket[k * lists + p], 0)
+            weight = jnp.where(valid, weight_ref[i], 0.0)
+            both = jnp.concatenate([key_ref[i], weight, jnp.zeros((6, CAP), F32)], axis=0)
+            turned = both.T
+            terms = jnp.where(turned[:, 0:1] == own_keys[k], turned[:, 1:2], 0.0)
+            added.append(totals[k] + jnp.sum(terms, axis=0, keepdims=True))
+        return tuple(added)
+
+    longest = functools.reduce(jnp.maximum, counts)
+    totals = lax.fori_loop(0, longest, add, (jnp.zeros((1, CAP), F32),) * LISTS)
+    for k in range(LISTS):
         place = pl.ds(k * CAP, CAP)
-        own_key = own_key_ref[k : k + 1, :]
-
-        def add(p, total):
-            i = bucket[k * lists + p]
-            both = jnp.concatenate([key_ref[i], weight_ref[i], jnp.zeros((6, CAP), F32)], axis=0)
-            turned = both.T
-            terms = jnp.where(turned[:, 0:1] == own_key, turned[:, 1:2], 0.0)
-            return total + jnp.sum(terms, axis=0, keepdims=True)
-
-        total = lax.fori_loop(0, counts[k], add, jnp.zeros((1, CAP), F32))
         weight = own_meta_ref[:, place].astype(F32)[3:4]
-        scaled = lifted_ref[:, place].astype(F32) * (weight / (1.0 + total))
+        scaled = lifted_ref[:, place].astype(F32) * (weight / (1.0 + totals[k]))
         term_ref[:, place] = scaled.astype(BF16)
 
 
-def forward_kernel(slab_ref, lifted_ref, meta_ref, tab_y_ref, tab_z_ref, tab_x_ref, modes_ref, wave_ref, total, lines, planes):
+def mix_modes(modes, weight_refs, spread_ref, collect_ref):
+    columns, own_modes = weight_refs[0].shape[0], weight_refs[0].shape[1]
+    depth, height = own_modes * 2 * C, own_modes * 2 * SIDE
+    lefts = []
+    for mode in modes:
+        sides = [nt_dot(spread_ref[i], mode) for i in range(spread_ref.shape[0])]
+        lefts.append(jnp.concatenate(sides, axis=1))
+    products = []
+    for left, weight_ref in zip(lefts, weight_refs):
+        blocks = []
+        for g in range(columns // SIDE):
+            weights = [weight_ref[SIDE * g + i].reshape(depth, C) for i in range(SIDE)]
+            rows = slice(height * g, height * (g + 1))
+            blocks.append(dot(left[rows].astype(BF16), jnp.concatenate(weights, axis=1)))
+        products.append(jnp.concatenate(blocks, axis=0).astype(BF16))
+    outs = []
+    for product in products:
+        turned = lax.dot_general(
+            product, collect_ref[...], (((0,), (0,)), ((), ())), preferred_element_type=F32
+        )
+        lane = lax.broadcasted_iota(jnp.int32, (C, turned.shape[1]), 1)
+        side = lane // own_modes % SIDE
+        total = turned[:C]
+        for i in range(1, SIDE):
+            total = jnp.where(side == i, turned[i * C : (i + 1) * C], total)
+        outs.append(total)
+    return outs
+
+
+def forward_kernel(
+    slab_ref, lifted_ref, meta_ref, tab_y_ref, tab_z_ref, tab_x_ref, spread_ref, collect_ref,
+    weight_ref, out_ref, wave_ref, total, lines, modes, weights, weight_sem, planes,
+):
     region = pl.program_id(0)
     rows = wave_ref.shape[1]
+    held = weights.shape[0]
+
+    def fetch(a, slot):
+        return pltpu.make_async_copy(weight_ref.at[a], weights.at[slot], weight_sem.at[slot])
 
     @pl.when(region == 0)
     def _():
+        for a in range(held):
+            fetch(a, a).start()
         total[...] = jnp.zeros_like(total)
 
     for k in range(LISTS):
@@ -318,31 +366,30 @@
 
         lax.fori_loop(0, C, along_x, 0, unroll=16)
         for a in range(M):
-            modes_ref[a] = lines[pl.ds(a, C, stride=M), :].astype(BF16)
-
-
-def mix_kernel(modes_ref, weight_ref, spread_ref, collect_ref, out_ref, products):
-    columns, own_modes = weight_ref.shape[1], weight_ref.shape[2]
-    depth, height = own_modes * 2 * C, own_modes * 2 * SIDE
-    modes = modes_ref[0]
-    sides = [nt_dot(spread_ref[i], modes) for i in range(spread_ref.shape[0])]
-    left = jnp.concatenate(sides, axis=1)
-    for g in range(columns // SIDE):
-        weights = [weight_ref[0, SIDE * g + i].reshape(depth, C) for i in range(SIDE)]
-        rows = slice(height * g, height * (g + 1))
-        products[rows, :] = dot(left[rows].astype(BF16), jnp.concatenate(weights, axis=1))
-    turned = lax.dot_general(
-        products[...].astype(BF16),
-        collect_ref[...],
-        (((0,), (0,)), ((), ())),
-        preferred_element_type=F32,
-    )
-    lane = lax.broadcasted_iota(jnp.int32, (C, turned.shape[1]), 1)
-    side = lane // own_modes % SIDE
-    total = turned[:C]
-    for i in range(1, SIDE):
-        total = jnp.where(side == i, turned[i * C : (i + 1) * C], total)
-    out_ref[0] = total
+            modes[a] = lines[pl.ds(a, C, stride=M), :].astype(BF16)
+
+        def mix(step, _):
+            first = step * STEP
+            places = [(first + i) % held for i in range(STEP)]
+            for i in range(STEP):
+                fetch(first + i, places[i]).wait()
+            outs = mix_modes(
+                [modes[first + i] for i in range(STEP)],
+                [weights.at[place] for place in places],
+                spread_ref,
+                collect_ref,
+            )
+            for i in range(STEP):
+                out_ref[first + i] = outs[i]
+
+            @pl.when(first + held < M)
+            def _():
+                for i in range(STEP):
+                    fetch(first + held + i, places[i]).start()
+
+            return 0
+
+        lax.fori_loop(0, M // STEP, mix, 0)
 
 
 def inverse_kernel(slab_ref, meta_ref, wave_ref, mixed_ref, tab_x_ref, out_ref, lines, field, planes):
@@ -379,19 +426,23 @@
 
 def cell_kernel(bucket, count, lifted_ref, key_ref, own_key_ref, out_ref):
     lists = key_ref.shape[0]
-    for k in range(LISTS):
-        own = own_key_ref[k : k + 1, :]
-        turned = jnp.broadcast_to(own, (8, CAP)).T[:, 0:1]
-
-        def add(p, total):
-            i = bucket[k * lists + p]
-            same = jnp.where(turned == key_ref[i], 1.0, 0.0).astype(BF16)
+    counts = [count[k] for k in range(LISTS)]
+    out_ref[...] = jnp.zeros_like(out_ref)
+    turned = [
+        jnp.broadcast_to(own_key_ref[k : k + 1, :], (8, CAP)).T[:, 0:1] for k in range(LISTS)
+    ]
+
+    def add(p, _):
+        for k in range(LISTS):
+            valid = p < counts[k]
+            i = jnp.where(valid, bucket[k * lists + p], 0)
+            key = jnp.where(valid, key_ref[i], -1.0)
+            same = jnp.where(turned[k] == key, 1.0, 0.0).astype(BF16)
             slots = pl.ds(pl.multiple_of((i % LISTS) * CAP, CAP), CAP)
-            return total + nt_dot(lifted_ref[i // LISTS, :, slots], same)
-
-        out_ref[:, pl.ds(k * CAP, CAP)] = lax.fori_loop(
-            0, count[k], add, jnp.zeros((C, CAP), F32)
-        )
+            out_ref[:, pl.ds(k * CAP, CAP)] += nt_dot(lifted_ref[i // LISTS, :, slots], same)
+        return 0
+
+    lax.fori_loop(0, functools.reduce(jnp.maximum, counts), add, 0)
 
 
 def decode_kernel(spectral_ref, cell_ref, meta_ref, point_ref, skip_ref, proj_ref, out_ref):
@@ -525,10 +576,11 @@
         return pl.BlockSpec(shape, lambda r, ids: (0,) * len(shape))
 
     tab_x = jnp.concatenate([cos_y, sin_y], 0)
-    modes, wave = pl.pallas_call(
+    spread, collect = selections(own_modes)
+    mixed, wave = pl.pallas_call(
         functools.partial(forward_kernel, planes=planes),
         out_shape=(
-            jax.ShapeDtypeStruct((M, C, rows), BF16),
+            jax.ShapeDtypeStruct((M, C, rows), F32),
             jax.ShapeDtypeStruct((slabs, rows, slots), BF16),
         ),
         grid_spec=pltpu.PrefetchScalarGridSpec(
@@ -540,30 +592,22 @@
                 whole((2 * rows, G)),
                 whole((2 * rows, G)),
                 whole((2 * M, G)),
+                whole(spread.shape),
+                whole(collect.shape),
+                pl.BlockSpec(memory_space=pl.ANY),
             ],
             out_specs=(whole((M, C, rows)), region_block(rows)),
-            scratch_shapes=[pltpu.VMEM((G * C, rows), F32), pltpu.VMEM((C * M, rows), F32)],
+            scratch_shapes=[
+                pltpu.VMEM((G * C, rows), F32),
+                pltpu.VMEM((C * M, rows), F32),
+                pltpu.VMEM((M, C, rows), BF16),
+                pltpu.VMEM((HELD,) + spectral_weight.shape[1:], BF16),
+                pltpu.SemaphoreType.DMA((HELD,)),
+            ],
         ),
-        compiler_params=params(),
+        compiler_params=params(VMEM_MOST),
         name="forward",
-    )(slab_ids, all_terms, all_meta, tab_y, tab_z, tab_x.astype(BF16))
-
-    spread, collect = selections(own_modes)
-    mixed = pl.pallas_call(
-        mix_kernel,
-        out_shape=jax.ShapeDtypeStruct((M, C, rows), F32),
-        grid=(M,),
-        in_specs=[
-            pl.BlockSpec((1, C, rows), lambda a: (a, 0, 0)),
-            pl.BlockSpec((1, M, own_modes, 2, C, C), lambda a: (a, 0, 0, 0, 0, 0)),
-            pl.BlockSpec(spread.shape, lambda a: (0, 0, 0)),
-            pl.BlockSpec(collect.shape, lambda a: (0, 0)),
-        ],
-        out_specs=pl.BlockSpec((1, C, rows), lambda a: (a, 0, 0)),
-        scratch_shapes=[pltpu.VMEM((2 * own_modes * M, SIDE * C), F32)],
-        compiler_params=params(),
-        name="mix",
-    )(modes, spectral_weight, spread, collect)
+    )(slab_ids, all_terms, all_meta, tab_y, tab_z, tab_x.astype(BF16), spread, collect, spectral_weight)
 
     partial = pl.pallas_call(
         functools.partial(inverse_kernel, planes=planes),

time: 191 us -> 168 us (0.88)
  Pallas kernels: 176 us -> 149 us
  local copies, waits for them, and re-layouts: 8.24 us -> 12.5 us
    pallas_call x1 -> x0, Pallas kernels: 38.9 us -> none  [shards(): pl.pallas_call(mix_kernel, out_shape=jax.ShapeDtypeStruct((M, C, rows), F...]
    pallas_call x1, Pallas kernels: 25.2 us -> 50.8 us  [shards(): pl.pallas_call(functools.partial(forward_kernel, planes=planes), out_shap...]
    pallas_call x1, Pallas kernels: 7.81 us -> 3.04 us  [shards(): pl.pallas_call(cell_kernel, out_shape=jax.ShapeDtypeStruct((C, slots), F3...]
    pallas_call x1, Pallas kernels: 10.5 us -> 5.89 us  [shards(): pl.pallas_call(share_kernel, out_shape=(jax.ShapeDtypeStruct((C, slots),...]
    pallas_call x1, Pallas kernels: 17.5 us -> 13 us  [shards(): pl.pallas_call(functools.partial(inverse_kernel, planes=planes), out_shap...]
    unnamed x26 -> x28, local copies, waits for them, and re-layouts: 5.39 us -> 9.09 us
where the time goes in v3:
time: 168 us; the launch traced here: 167 us
  Pallas kernels  149 us (89%)
  local copies, waits for them, and re-layouts  12.5 us (7%)
  other arithmetic  5.47 us (3%)
    pallas_call x1, Pallas kernels, shards(): pl.pallas_call(functools.partial(forward_kernel, planes=planes), out_shap...  50.8 us
    pallas_call x2, Pallas kernels, gather(): pl.pallas_call(functools.partial(gather_kernel, depth=depth, width=width)...  40.6 us
    pallas_call x1, Pallas kernels, scatter(): pl.pallas_call(functools.partial(scatter_kernel, depth=depth, width=width...  28.8 us
    pallas_call x1, Pallas kernels, shards(): pl.pallas_call(functools.partial(inverse_kernel, planes=planes), out_shap...  13 us
    unnamed x28, local copies, waits for them, and re-layouts  9.09 us
    pallas_call x1, Pallas kernels, shards(): pl.pallas_call(share_kernel, out_shape=(jax.ShapeDtypeStruct((C, slots),...  5.89 us
    pallas_call x1, Pallas kernels, shards(): pl.pallas_call(functools.partial(prep_kernel, planes=planes), out_shape=(...  3.7 us

profile of v3, /device:TPU:0, one launch (start us, length us, event | category | flops | bytes accessed | tf_op | source)
XLA Modules:
  0.0 167.2 jit_solution(17917432822080010326)
XLA Ops:
  0.0 0.1 cosine_convert_fusion
  0.1 0.8 fusion.15
  1.0 0.1 add_reduce_fusion
  1.1 0.1 select_reduce_fusion.2.own_slab_ref
  1.2 0.1 concatenate.28.slab_ref
  1.3 0.1 fusion.4
  1.4 0.7 add_bitcast_fusion.1
  2.1 0.7 add_bitcast_fusion
  2.8 0.1 select_reduce_fusion
  3.0 0.1 copy.27
  3.1 0.3 multiply_cosine_fusion
  3.4 0.1 copy.28
  3.5 0.1 copy.30
  3.6 0.1 copy.29
  3.7 0.7 pad_maximum_fusion
  4.4 0.1 fusion.2
  4.5 0.1 fusion.1.tab_x_ref
  4.6 0.7 copy.31.tab_x_ref
  5.3 0.0 copy-start.6
  5.3 0.9 copy-done.6
  6.2 0.0 copy-start.8
  6.2 0.8 copy-done.8
  7.0 0.0 copy-start.11
  7.0 0.7 copy-done.11
  7.7 3.7 %prep.1 = (bf16[64,1280]{1,0:T(8,128)(2,1)S(1)}, bf16[16,1280]{1,0:T(8,128)(2,1)S(1)}) custom-call(bf16[64,2048]{1,0:T(8,128)(2,1)S(1)} %bitcast.22, f32[3,2048]{1,0:T(4,128)S(1)} %copy-done.8, s32[8,256]{1,0:T(8,128)S(1)} %concatenate.25.point_ref, s32[8,256]{1,0:T(8,128)S(1)} %concatenate.26.cell_ref, s32[8,256]{1,0:T(8,128)S(1)} %concatenate.28.slab_ref, ...), custom_call_target="tpu_custom_call" | custom-call | tf_op jit(solution)/shard_map/prep/pallas_call | solution.py:528
  11.4 0.0 copy-start.4
  11.5 0.5 copy-done.4
  12.0 15.2 %gather_meta.1.meta_ref = bf16[16,16,1280]{2,1,0:T(8,128)(2,1)} custom-call(bf16[16,1280]{1,0:T(8,128)(2,1)} %copy-done.4), custom_call_target="tpu_custom_call" | custom-call | tf_op jit(solution)/shard_map/gather_meta/pallas_call | solution.py:164
  27.2 0.0 copy-start.5
  27.2 1.1 slice.28
  28.4 0.1 reshape.230
  28.5 0.0 copy-start.12
  28.5 1.1 slice.32
  29.5 0.1 convert.36.weight_ref
  29.6 1.2 convert_element_type.79
  30.8 0.2 slice_add_fusion
  31.0 0.0 copy-done.5
  31.0 5.9 %share.1 = (bf16[64,1280]{1,0:T(8,128)(2,1)S(1)}, s32[480]{0:T(512)S(1)}, s32[5]{0:T(128)S(1)}) custom-call(s32[80]{0:T(128)S(1)} %and_select_fusion.1.slab_ref, s32[5]{0:T(128)S(1)} %select_reduce_fusion.2.own_slab_ref, f32[80,1,256]{2,1,0:T(1,128)S(1)} %bitcast.20, f32[80,1,256]{2,1,0:T(1,128)S(1)} %convert.36.weight_ref, ...), custom_call_target="tpu_custom_call" | custom-call | tf_op jit(solution)/shard_map/share/pallas_call | solution.py:551
  36.9 0.0 copy-start.7
  37.0 0.7 copy-done.7
  37.6 25.4 %gather_terms.1.lifted_ref = bf16[16,64,1280]{2,1,0:T(8,128)(2,1)} custom-call(bf16[64,1280]{1,0:T(8,128)(2,1)} %copy-done.7), custom_call_target="tpu_custom_call" | custom-call | tf_op jit(solution)/shard_map/gather_terms/pallas_call | solution.py:164
  63.0 0.0 copy-done.12
  63.0 0.0 copy-start
  63.0 1.7 %copy-done = bf16[16,64,1280]{2,1,0:T(8,128)(2,1)S(1)} copy-done((bf16[16,64,1280]{2,1,0:T(8,128)(2,1)S(1)}, bf16[16,64,1280]{2,1,0:T(8,128)(2,1)}, u32[]{:S(2)}) %copy-start) | copy-done | bytes 2621464
  64.7 3.0 %cells.1.cell_ref = f32[64,1280]{1,0:T(8,128)S(1)} custom-call(s32[480]{0:T(512)S(1)} %get-tuple-element.17.bucket, s32[5]{0:T(128)S(1)} %get-tuple-element.18.count, bf16[16,64,1280]{2,1,0:T(8,128)(2,1)S(1)} %copy-done, f32[80,1,256]{2,1,0:T(1,128)S(1)} %bitcast.21, f32[8,256]{1,0:T(8,128)S(1)} %concatenate.29.own_key_ref), custom_call_target="tpu_custom_call" | custom-call | tf_op jit(solution)/shard_map/cells/pallas_call | solution.py:632
  67.8 0.0 copy-start.1
  67.8 0.0 copy-start.13
  67.8 50.8 %forward.1 = (f32[32,64,128]{2,1,0:T(8,128)}, bf16[16,128,1280]{2,1,0:T(8,128)(2,1)}) custom-call(s32[80]{0:T(128)} %copy-done.12, bf16[16,64,1280]{2,1,0:T(8,128)(2,1)} %gather_terms.1.lifted_ref, bf16[16,16,1280]{2,1,0:T(8,128)(2,1)} %gather_meta.1.meta_ref, bf16[256,128]{1,0:T(8,128)(2,1)} %get-tuple-element.32.tab_y_ref, ...), custom_call_target="tpu_custom_call" | custom-call | tf_op jit(solution)/shard_map/forward/pallas_call | solution.py:580
  118.6 0.0 copy-done.1
  118.6 0.0 copy-done.13
  118.6 0.0 copy-start.2
  118.6 2.5 %copy-done.2 = bf16[16,128,1280]{2,1,0:T(8,128)(2,1)S(1)} copy-done((bf16[16,128,1280]{2,1,0:T(8,128)(2,1)S(1)}, bf16[16,128,1280]{2,1,0:T(8,128)(2,1)}, u32[]{:S(2)}) %copy-start.2) | copy-done | bytes 5242904
  121.1 0.0 copy-start.3
  121.1 1.2 copy-done.3
  122.3 13.0 %inverse.1.blocks_ref = bf16[16,64,1280]{2,1,0:T(8,128)(2,1)S(1)} custom-call(s32[80]{0:T(128)S(1)} %copy-done.13, bf16[16,16,1280]{2,1,0:T(8,128)(2,1)S(1)} %copy-done.1, bf16[16,128,1280]{2,1,0:T(8,128)(2,1)S(1)} %copy-done.2, f32[2048,128]{1,0:T(8,128)S(1)} %bitcast.19, bf16[128,64]{1,0:T(8,128)(2,1)S(1)} %fusion.1.tab_x_ref), custom_call_target="tpu_custom_call" | custom-call | tf_op jit(solution)/shard_map/inverse/pallas_call | solution.py:612
  135.3 0.0 copy-start.9
  135.4 0.0 copy-start.10
  135.4 28.8 %scatter.1.spectral_ref = f32[64,1280]{1,0:T(8,128)S(1)} custom-call(bf16[16,64,1280]{2,1,0:T(8,128)(2,1)S(1)} %inverse.1.blocks_ref), custom_call_target="tpu_custom_call" | custom-call | tf_op jit(solution)/shard_map/scatter/pallas_call | solution.py:234
  164.1 0.0 copy-done.9
  164.2 0.0 copy-done.10
  164.2 3.0 %decode.1 = bf16[64,2048]{1,0:T(8,128)(2,1)} custom-call(f32[64,1280]{1,0:T(8,128)S(1)} %scatter.1.spectral_ref, f32[64,1280]{1,0:T(8,128)S(1)} %cells.1.cell_ref, bf16[16,1280]{1,0:T(8,128)(2,1)S(1)} %copy-done.5, s32[8,256]{1,0:T(8,128)S(1)} %concatenate.25.point_ref, bf16[64,64]{1,0:T(8,128)(2,1)S(1)} %copy-done.9, bf16[64,64]{1,0:T(8,128)(2,1)S(1)} %copy-done.10), custom_call_target="tpu_custom_call" | custom-call | tf_op jit(solution)/shard_map/decode/pallas_call | solution.py:641
  (20 shorter events, 0.3 us)
Async XLA Ops:
  5.3 0.9 copy-start.6
  6.2 0.8 copy-start.8
  7.0 0.7 copy-start.11
  11.4 0.6 copy-start.4
  27.2 3.8 %copy-start.5 = (bf16[16,1280]{1,0:T(8,128)(2,1)S(1)}, bf16[16,1280]{1,0:T(8,128)(2,1)}, u32[]{:S(2)}) copy-start(bf16[16,1280]{1,0:T(8,128)(2,1)} %copy-done.4) | copy-start | bytes 122884
  28.5 34.5 %copy-start.12 = (s32[80]{0:T(128)}, s32[80]{0:T(128)S(1)}, u32[]{:S(2)}) copy-start(s32[80]{0:T(128)S(1)} %and_select_fusion.1.slab_ref) | copy-start | bytes 964
  36.9 0.7 copy-start.7
  63.0 1.7 %copy-start = (bf16[16,64,1280]{2,1,0:T(8,128)(2,1)S(1)}, bf16[16,64,1280]{2,1,0:T(8,128)(2,1)}, u32[]{:S(2)}) copy-start(bf16[16,64,1280]{2,1,0:T(8,128)(2,1)} %gather_terms.1.lifted_ref) | copy-start | bytes 7864324
  67.8 50.8 %copy-start.1 = (bf16[16,16,1280]{2,1,0:T(8,128)(2,1)S(1)}, bf16[16,16,1280]{2,1,0:T(8,128)(2,1)}, u32[]{:S(2)}) copy-start(bf16[16,16,1280]{2,1,0:T(8,128)(2,1)} %gather_meta.1.meta_ref) | copy-start | bytes 1966084
  67.8 50.8 %copy-start.13 = (s32[80]{0:T(128)S(1)}, s32[80]{0:T(128)}, u32[]{:S(2)}) copy-start(s32[80]{0:T(128)} %copy-done.12) | copy-start | bytes 964
  118.6 2.5 %copy-start.2 = (bf16[16,128,1280]{2,1,0:T(8,128)(2,1)S(1)}, bf16[16,128,1280]{2,1,0:T(8,128)(2,1)}, u32[]{:S(2)}) copy-start(bf16[16,128,1280]{2,1,0:T(8,128)(2,1)} %get-tuple-element.15.wave_ref) | copy-start | bytes 15728644
  121.1 1.2 copy-start.3
  135.3 28.8 %copy-start.9 = (bf16[64,64]{1,0:T(8,128)(2,1)S(1)}, bf16[64,64]{1,0:T(8,128)(2,1)}, u32[]{:S(2)}) copy-start(bf16[64,64]{1,0:T(8,128)(2,1)} %skip_ref.1) | copy-start | bytes 24580
  135.4 28.8 %copy-start.10 = (bf16[64,64]{1,0:T(8,128)(2,1)S(1)}, bf16[64,64]{1,0:T(8,128)(2,1)}, u32[]{:S(2)}) copy-start(bf16[64,64]{1,0:T(8,128)(2,1)} %proj_ref.1) | copy-start | bytes 24580

commit v4 on v3

--- a/solution.py
+++ b/solution.py
@@ -177,8 +177,8 @@
 
 
 def scatter_kernel(
-    blocks_ref, out_ref, from_core, from_y, from_z, to_y, to_z,
-    core_send, core_recv, y_send, y_recv, z_send, z_recv, depth, width,
+    slab_ref, meta_ref, wave_ref, field_ref, out_ref, blocks, from_core, from_y, from_z, to_y, to_z,
+    core_send, core_recv, y_send, y_recv, z_send, z_recv, depth, width, planes,
 ):
     at, z, y, core = peers(depth, width)
     ahead = [at((z + d) % depth, y, core) for d in range(1, depth)]
@@ -187,27 +187,43 @@
     greet(ahead + ([beside] if width > 1 else []) + [twin])
     order = list(range(1, depth)) + [0]
     core_copies, y_copies, z_copies = {}, {}, {}
-    for d in order:
-        for w in reversed(range(width)):
+
+    def evaluate(d):
+        def one(j, _):
+            block = at((z + d) % depth, (y + j) % width, (core + 1 + j // width) % 2)
+            for k in range(LISTS):
+                place = pl.ds(k * CAP, CAP)
+                slab = slab_ref[block * LISTS + k]
+                local = meta_ref[block, :, place].astype(F32)[0:1] - (slab * planes).astype(F32)
+                values = dot(field_ref[slab], wave_ref[block, :, place])
+                total = values[:C]
+                for p in range(1, planes):
+                    total = jnp.where(local == float(p), values[p * C : (p + 1) * C], total)
+                blocks[block, :, place] = total.astype(BF16)
+            return 0
+
+        lax.fori_loop(0, 2 * width, one, 0)
+        for w in range(width):
             slot = d * width + w
             target = at((z + d) % depth, (y + w) % width, 1 - core)
             core_copies[slot] = remote(
-                blocks_ref.at[target], from_core.at[slot], core_send.at[slot], core_recv.at[slot], twin
+                blocks.at[target], from_core.at[slot], core_send.at[slot], core_recv.at[slot], twin
             )
             core_copies[slot].start()
 
     def pair(d, w):
         slot = d * width + w
         core_copies[slot].wait_recv()
-        own = blocks_ref[at((z + d) % depth, (y + w) % width, core)].astype(F32)
+        own = blocks[at((z + d) % depth, (y + w) % width, core)].astype(F32)
         return own + from_core[slot].astype(F32)
 
-    if width > 1:
-        for d in order:
+    def along_y(d):
+        if width > 1:
             to_y[d] = pair(d, 1).astype(BF16)
             y_copies[d] = remote(to_y.at[d], from_y.at[d], y_send.at[d], y_recv.at[d], beside)
             y_copies[d].start()
-    for d in order:
+
+    def along_z(d):
         total = pair(d, 0)
         if width > 1:
             y_copies[d].wait_recv()
@@ -220,6 +236,14 @@
             z_copies[d].start()
         else:
             out_ref[...] = total
+
+    for n in range(depth + 2):
+        if n < depth:
+            evaluate(order[n])
+        if 0 <= n - 1 < depth:
+            along_y(order[n - 1])
+        if 0 <= n - 2 < depth:
+            along_z(order[n - 2])
     for d in range(1, depth):
         z_copies[d].wait_recv()
         out_ref[...] += from_z[d].astype(F32)
@@ -228,15 +252,17 @@
             copy.wait_send()
 
 
-def scatter(blocks, slabs, collective_id, name):
+def scatter(slab_ids, meta, wave, field, planes, collective_id, name):
+    slabs, slots = meta.shape[0], meta.shape[2]
     depth, width = places(slabs)
-    shape = blocks.shape[1:]
+    shape = (C, slots)
     return pl.pallas_call(
-        functools.partial(scatter_kernel, depth=depth, width=width),
+        functools.partial(scatter_kernel, depth=depth, width=width, planes=planes),
         out_shape=jax.ShapeDtypeStruct(shape, F32),
-        in_specs=[VMEM],
+        in_specs=[SMEM, VMEM, VMEM, VMEM],
         out_specs=VMEM,
         scratch_shapes=[
+            pltpu.VMEM((slabs,) + shape, BF16),
             pltpu.VMEM((depth * width,) + shape, BF16),
             *[pltpu.VMEM((depth,) + shape, BF16)] * 4,
             *[pltpu.SemaphoreType.DMA((depth * width,))] * 2,
@@ -246,7 +272,7 @@
             collective_id=collective_id, has_side_effects=True, vmem_limit_bytes=VMEM_LIMIT
         ),
         name=name,
-    )(blocks)
+    )(slab_ids, meta, wave, field)
 
 
 def share_kernel(slab_ref, own_slab_ref, key_ref, weight_ref, own_key_ref, own_meta_ref, lifted_ref, term_ref, bucket, count):
@@ -316,7 +342,7 @@
 
 def forward_kernel(
     slab_ref, lifted_ref, meta_ref, tab_y_ref, tab_z_ref, tab_x_ref, spread_ref, collect_ref,
-    weight_ref, out_ref, wave_ref, total, lines, modes, weights, weight_sem, planes,
+    tab_back_ref, weight_ref, field_ref, wave_ref, total, lines, modes, weights, weight_sem, planes,
 ):
     region = pl.program_id(0)
     rows = wave_ref.shape[1]
@@ -380,7 +406,8 @@
                 collect_ref,
             )
             for i in range(STEP):
-                out_ref[first + i] = outs[i]
+                at = pl.ds(pl.multiple_of((first + i) * C, C), C)
+                lines[at, :] = outs[i]
 
             @pl.when(first + held < M)
             def _():
@@ -391,37 +418,15 @@
 
         lax.fori_loop(0, M // STEP, mix, 0)
 
-
-def inverse_kernel(slab_ref, meta_ref, wave_ref, mixed_ref, tab_x_ref, out_ref, lines, field, planes):
-    region = pl.program_id(0)
-    rows = wave_ref.shape[1]
-    height = planes * C
-
-    @pl.when(region == 0)
-    def _():
-        half = rows // 2
-        sign = jnp.where(lax.broadcasted_iota(jnp.int32, (M, rows), 1) < half, -1.0, 1.0)
-
-        def along_x(e, _):
-            line = mixed_ref[pl.ds(e, M, stride=C), :]
-            turned = sign * jnp.concatenate([line[:, half:], line[:, :half]], axis=1)
+        def back_along_x(e, _):
+            line = lines[pl.ds(e, M, stride=C), :]
+            turned = -sign * jnp.concatenate([line[:, half:], line[:, :half]], axis=1)
             both = jnp.concatenate([line, turned], axis=0).astype(BF16)
-            lines[pl.ds(e, G, stride=C), :] = dot(tab_x_ref[...], both)
+            total[pl.ds(e, G, stride=C), :] = dot(tab_back_ref[...], both)
             return 0
 
-        lax.fori_loop(0, C, along_x, 0, unroll=16)
-        field[...] = lines[...].astype(BF16)
-
-    for k in range(LISTS):
-        place = pl.ds(k * CAP, CAP)
-        slab = slab_ref[region * LISTS + k]
-        local = meta_ref[0, :, place].astype(F32)[0:1] - (slab * planes).astype(F32)
-        at = pl.ds(pl.multiple_of(slab * height, height), height)
-        values = dot(field[at, :], wave_ref[0, :, place])
-        total = jnp.zeros((C, CAP), F32)
-        for p in range(planes):
-            total += jnp.where(local == float(p), values[p * C : (p + 1) * C], 0.0)
-        out_ref[0, :, place] = total.astype(BF16)
+        lax.fori_loop(0, C, back_along_x, 0, unroll=16)
+        field_ref[...] = total[...].astype(BF16).reshape(field_ref.shape)
 
 
 def cell_kernel(bucket, count, lifted_ref, key_ref, own_key_ref, out_ref):
@@ -576,11 +581,12 @@
         return pl.BlockSpec(shape, lambda r, ids: (0,) * len(shape))
 
     tab_x = jnp.concatenate([cos_y, sin_y], 0)
+    tab_back = (tab_x.T / float(G * G * G)).astype(BF16)
     spread, collect = selections(own_modes)
-    mixed, wave = pl.pallas_call(
+    field, wave = pl.pallas_call(
         functools.partial(forward_kernel, planes=planes),
         out_shape=(
-            jax.ShapeDtypeStruct((M, C, rows), F32),
+            jax.ShapeDtypeStruct((slabs, planes * C, rows), BF16),
             jax.ShapeDtypeStruct((slabs, rows, slots), BF16),
         ),
         grid_spec=pltpu.PrefetchScalarGridSpec(
@@ -594,9 +600,10 @@
                 whole((2 * M, G)),
                 whole(spread.shape),
                 whole(collect.shape),
+                whole((G, 2 * M)),
                 pl.BlockSpec(memory_space=pl.ANY),
             ],
-            out_specs=(whole((M, C, rows)), region_block(rows)),
+            out_specs=(whole((slabs, planes * C, rows)), region_block(rows)),
             scratch_shapes=[
                 pltpu.VMEM((G * C, rows), F32),
                 pltpu.VMEM((C * M, rows), F32),
@@ -607,27 +614,9 @@
         ),
         compiler_params=params(VMEM_MOST),
         name="forward",
-    )(slab_ids, all_terms, all_meta, tab_y, tab_z, tab_x.astype(BF16), spread, collect, spectral_weight)
-
-    partial = pl.pallas_call(
-        functools.partial(inverse_kernel, planes=planes),
-        out_shape=jax.ShapeDtypeStruct((slabs, C, slots), BF16),
-        grid_spec=pltpu.PrefetchScalarGridSpec(
-            num_scalar_prefetch=1,
-            grid=(slabs,),
-            in_specs=[
-                region_block(16),
-                region_block(rows),
-                whole((M * C, rows)),
-                whole((G, 2 * M)),
-            ],
-            out_specs=region_block(C),
-            scratch_shapes=[pltpu.VMEM((G * C, rows), F32), pltpu.VMEM((G * C, rows), BF16)],
-        ),
-        compiler_params=params(),
-        name="inverse",
-    )(slab_ids, all_meta, wave, mixed.reshape(M * C, rows), (tab_x.T / float(G * G * G)).astype(BF16))
-    spectral = scatter(partial, slabs, 2, "scatter")
+    )(slab_ids, all_terms, all_meta, tab_y, tab_z, tab_x.astype(BF16), spread, collect, tab_back, spectral_weight)
+
+    spectral = scatter(slab_ids, all_meta, wave, field, planes, 2, "scatter")
 
     cell_lifted = pl.pallas_call(
         cell_kernel,

time: 168 us -> 161 us (0.958)
  Pallas kernels: 149 us -> 143 us
    pallas_call x1 -> x0, Pallas kernels: 13 us -> none  [shards(): pl.pallas_call(functools.partial(inverse_kernel, planes=planes), out_shap...]
    pallas_call x1, Pallas kernels: 50.8 us -> 55.6 us  [shards(): pl.pallas_call(functools.partial(forward_kernel, planes=planes), out_shap...]
    pallas_call x1, Pallas kernels: 28.8 us -> 31 us  [scatter(): pl.pallas_call(functools.partial(scatter_kernel, depth=depth, width=width...]
where the time goes in v4:
time: 161 us; the launch traced here: 160 us
  Pallas kernels  143 us (89%)
  local copies, waits for them, and re-layouts  11.3 us (7%)
  other arithmetic  6.08 us (4%)
    pallas_call x1, Pallas kernels, shards(): pl.pallas_call(functools.partial(forward_kernel, planes=planes), out_shap...  55.6 us
    pallas_call x2, Pallas kernels, gather(): pl.pallas_call(functools.partial(gather_kernel, depth=depth, width=width)...  40.6 us
    pallas_call x1, Pallas kernels, scatter(): pl.pallas_call(functools.partial(scatter_kernel, depth=depth, width=width...  31 us
    unnamed x28, local copies, waits for them, and re-layouts  7.8 us
    pallas_call x1, Pallas kernels, shards(): pl.pallas_call(share_kernel, out_shape=(jax.ShapeDtypeStruct((C, slots),...  6.07 us
    pallas_call x1, Pallas kernels, shards(): pl.pallas_call(functools.partial(prep_kernel, planes=planes), out_shape=(...  3.7 us

profile of v4, /device:TPU:0, one launch (start us, length us, event | category | flops | bytes accessed | tf_op | source)
XLA Modules:
  0.0 160.5 jit_solution(13780722040309644918)
XLA Ops:
  0.0 0.7 add_bitcast_fusion
  0.7 0.8 fusion.15
  1.6 0.1 add_reduce_fusion
  1.7 0.7 add_bitcast_fusion.1
  2.4 0.1 select_reduce_fusion
  2.6 0.1 select_reduce_fusion.2.own_slab_ref
  2.7 0.1 concatenate.28.slab_ref
  2.8 0.0 copy-start.6
  2.8 1.0 copy-done.6
  3.7 0.0 copy-start.8
  3.7 0.8 copy-done.8
  4.5 0.0 copy-start.11
  4.5 0.7 copy-done.11
  5.2 3.7 %prep.1 = (bf16[64,1280]{1,0:T(8,128)(2,1)S(1)}, bf16[16,1280]{1,0:T(8,128)(2,1)S(1)}) custom-call(bf16[64,2048]{1,0:T(8,128)(2,1)S(1)} %bitcast.20, f32[3,2048]{1,0:T(4,128)S(1)} %copy-done.8, s32[8,256]{1,0:T(8,128)S(1)} %concatenate.25.point_ref, s32[8,256]{1,0:T(8,128)S(1)} %concatenate.26.cell_ref, s32[8,256]{1,0:T(8,128)S(1)} %concatenate.28.slab_ref, ...), custom_call_target="tpu_custom_call" | custom-call | tf_op jit(solution)/shard_map/prep/pallas_call | solution.py:533
  8.9 0.0 copy-start.4
  8.9 0.6 copy-done.4
  9.5 0.0 copy-start.5
  9.5 15.2 %gather_meta.1.meta_ref = bf16[16,16,1280]{2,1,0:T(8,128)(2,1)} custom-call(bf16[16,1280]{1,0:T(8,128)(2,1)} %copy-done.4), custom_call_target="tpu_custom_call" | custom-call | tf_op jit(solution)/shard_map/gather_meta/pallas_call | solution.py:164
  24.7 1.1 slice.28
  25.9 0.1 reshape.226
  26.0 0.0 copy-start.12
  26.0 1.2 convert_element_type.79
  27.2 0.2 slice_add_fusion
  27.4 1.1 slice.32
  28.4 0.1 convert.36.weight_ref
  28.5 0.0 copy-done.5
  28.6 6.1 %share.1 = (bf16[64,1280]{1,0:T(8,128)(2,1)S(1)}, s32[480]{0:T(512)S(1)}, s32[5]{0:T(128)S(1)}) custom-call(s32[80]{0:T(128)S(1)} %and_select_fusion.1.slab_ref, s32[5]{0:T(128)S(1)} %select_reduce_fusion.2.own_slab_ref, f32[80,1,256]{2,1,0:T(1,128)S(1)} %bitcast.18, f32[80,1,256]{2,1,0:T(1,128)S(1)} %convert.36.weight_ref, ...), custom_call_target="tpu_custom_call" | custom-call | tf_op jit(solution)/shard_map/share/pallas_call | solution.py:556
  34.7 0.0 copy-start.7
  34.7 0.7 copy-done.7
  35.4 25.4 %gather_terms.1.lifted_ref = bf16[16,64,1280]{2,1,0:T(8,128)(2,1)} custom-call(bf16[64,1280]{1,0:T(8,128)(2,1)} %copy-done.7), custom_call_target="tpu_custom_call" | custom-call | tf_op jit(solution)/shard_map/gather_terms/pallas_call | solution.py:164
  60.7 0.0 copy-done.12
  60.8 0.1 fusion.4
  60.8 0.1 copy.27
  60.9 0.3 multiply_cosine_fusion
  61.2 0.1 copy.30
  61.3 0.1 copy.29
  61.4 0.1 copy.28
  61.5 0.1 cosine_convert_fusion
  61.7 0.7 pad_maximum_fusion
  62.4 0.1 fusion.2
  62.5 0.7 copy.31.tab_x_ref
  63.1 0.7 fusion.1.tab_back_ref
  63.8 0.0 copy-start.1
  63.8 0.0 copy-start.13
  63.8 55.6 %forward.1 = (bf16[16,512,128]{2,1,0:T(8,128)(2,1)}, bf16[16,128,1280]{2,1,0:T(8,128)(2,1)}) custom-call(s32[80]{0:T(128)} %copy-done.12, bf16[16,64,1280]{2,1,0:T(8,128)(2,1)} %gather_terms.1.lifted_ref, bf16[16,16,1280]{2,1,0:T(8,128)(2,1)} %gather_meta.1.meta_ref, bf16[256,128]{1,0:T(8,128)(2,1)} %get-tuple-element.32.tab_y_ref, ...), custom_call_target="tpu_custom_call" | custom-call | tf_op jit(solution)/shard_map/forward/pallas_call | solution.py:586
  119.4 0.0 copy-done.1
  119.4 0.0 copy-done.13
  119.4 0.0 copy-start.2
  119.4 2.5 %copy-done.2 = bf16[16,128,1280]{2,1,0:T(8,128)(2,1)S(1)} copy-done((bf16[16,128,1280]{2,1,0:T(8,128)(2,1)S(1)}, bf16[16,128,1280]{2,1,0:T(8,128)(2,1)}, u32[]{:S(2)}) %copy-start.2) | copy-done | bytes 5242904
  121.9 0.0 copy-start.3
  121.9 1.6 copy-done.3
  123.5 0.0 copy-start
  123.5 31.0 %scatter.1.spectral_ref = f32[64,1280]{1,0:T(8,128)S(1)} custom-call(s32[80]{0:T(128)S(1)} %copy-done.13, bf16[16,16,1280]{2,1,0:T(8,128)(2,1)S(1)} %copy-done.1, bf16[16,128,1280]{2,1,0:T(8,128)(2,1)S(1)} %copy-done.2, bf16[16,512,128]{2,1,0:T(8,128)(2,1)S(1)} %copy-done.3), custom_call_target="tpu_custom_call" | custom-call | tf_op jit(solution)/shard_map/scatter/pallas_call | solution.py:259
  154.5 0.0 copy-start.9
  154.5 0.0 copy-start.10
  154.6 0.0 copy-done
  154.6 2.9 %cells.1.cell_ref = f32[64,1280]{1,0:T(8,128)S(1)} custom-call(s32[480]{0:T(512)S(1)} %get-tuple-element.17.bucket, s32[5]{0:T(128)S(1)} %get-tuple-element.18.count, bf16[16,64,1280]{2,1,0:T(8,128)(2,1)S(1)} %copy-done, f32[80,1,256]{2,1,0:T(1,128)S(1)} %bitcast.19, f32[8,256]{1,0:T(8,128)S(1)} %concatenate.29.own_key_ref), custom_call_target="tpu_custom_call" | custom-call | tf_op jit(solution)/shard_map/cells/pallas_call | solution.py:621
  157.5 0.0 copy-done.9
  157.5 0.0 copy-done.10
  157.5 3.0 %decode.1 = bf16[64,2048]{1,0:T(8,128)(2,1)} custom-call(f32[64,1280]{1,0:T(8,128)S(1)} %scatter.1.spectral_ref, f32[64,1280]{1,0:T(8,128)S(1)} %cells.1.cell_ref, bf16[16,1280]{1,0:T(8,128)(2,1)S(1)} %copy-done.5, s32[8,256]{1,0:T(8,128)S(1)} %concatenate.25.point_ref, bf16[64,64]{1,0:T(8,128)(2,1)S(1)} %copy-done.9, bf16[64,64]{1,0:T(8,128)(2,1)S(1)} %copy-done.10), custom_call_target="tpu_custom_call" | custom-call | tf_op jit(solution)/shard_map/decode/pallas_call | solution.py:630
  (20 shorter events, 0.3 us)
Async XLA Ops:
  2.8 1.0 copy-start.6
  3.7 0.8 copy-start.8
  4.5 0.7 copy-start.11
  8.9 0.6 copy-start.4
  9.5 19.0 %copy-start.5 = (bf16[16,1280]{1,0:T(8,128)(2,1)S(1)}, bf16[16,1280]{1,0:T(8,128)(2,1)}, u32[]{:S(2)}) copy-start(bf16[16,1280]{1,0:T(8,128)(2,1)} %copy-done.4) | copy-start | bytes 122884
  26.0 34.8 %copy-start.12 = (s32[80]{0:T(128)}, s32[80]{0:T(128)S(1)}, u32[]{:S(2)}) copy-start(s32[80]{0:T(128)S(1)} %and_select_fusion.1.slab_ref) | copy-start | bytes 964
  34.7 0.7 copy-start.7
  63.8 55.6 %copy-start.1 = (bf16[16,16,1280]{2,1,0:T(8,128)(2,1)S(1)}, bf16[16,16,1280]{2,1,0:T(8,128)(2,1)}, u32[]{:S(2)}) copy-start(bf16[16,16,1280]{2,1,0:T(8,128)(2,1)} %gather_meta.1.meta_ref) | copy-start | bytes 1966084
  63.8 55.6 %copy-start.13 = (s32[80]{0:T(128)S(1)}, s32[80]{0:T(128)}, u32[]{:S(2)}) copy-start(s32[80]{0:T(128)} %copy-done.12) | copy-start | bytes 964
  119.4 2.5 %copy-start.2 = (bf16[16,128,1280]{2,1,0:T(8,128)(2,1)S(1)}, bf16[16,128,1280]{2,1,0:T(8,128)(2,1)}, u32[]{:S(2)}) copy-start(bf16[16,128,1280]{2,1,0:T(8,128)(2,1)} %get-tuple-element.15.wave_ref) | copy-start | bytes 15728644
  121.9 1.6 copy-start.3
  123.5 31.0 %copy-start = (bf16[16,64,1280]{2,1,0:T(8,128)(2,1)S(1)}, bf16[16,64,1280]{2,1,0:T(8,128)(2,1)}, u32[]{:S(2)}) copy-start(bf16[16,64,1280]{2,1,0:T(8,128)(2,1)} %gather_terms.1.lifted_ref) | copy-start | bytes 7864324
  154.5 2.9 %copy-start.9 = (bf16[64,64]{1,0:T(8,128)(2,1)S(1)}, bf16[64,64]{1,0:T(8,128)(2,1)}, u32[]{:S(2)}) copy-start(bf16[64,64]{1,0:T(8,128)(2,1)} %skip_ref.1) | copy-start | bytes 24580
  154.5 2.9 %copy-start.10 = (bf16[64,64]{1,0:T(8,128)(2,1)S(1)}, bf16[64,64]{1,0:T(8,128)(2,1)}, u32[]{:S(2)}) copy-start(bf16[64,64]{1,0:T(8,128)(2,1)} %proj_ref.1) | copy-start | bytes 24580
